TPU v7x, 512 devices: a whole 4x8x8 slice. The times are simulated.
512 devices in a mesh: dp: 256 (over z, y, x), ctx: 2 (over core).
Axes of the slice: x: 4, y: 8, z: 8, core: 2. Of those that a mesh axis runs over, the one named last changes fastest.
Arguments:
- query_rows: bfloat16 [65536, 1024], P(('dp', 'ctx')), may hold values from -6 to 6
- key_rows: bfloat16 [65536, 1024], P(('dp', 'ctx')), may hold values from -6 to 6
- value_rows: bfloat16 [65536, 1024], P(('dp', 'ctx')), may hold values from -6 to 6
- gate_rows: bfloat16 [65536, 1024], P(('dp', 'ctx')), may hold values from -6 to 6
- lengths: int32 [256, 4], P('dp'), may hold values from 1 to 128, 256 in all within a row
- norm_gain: float32 [1024], replicated, may hold values from 0.3 to 3
- out_weight: bfloat16 [1024, 1024], replicated, may hold values from -0.1875 to 0.1875
- cotangent: bfloat16 [65536, 1024], P(('dp', 'ctx')), may hold values from -6 to 6
Outputs:
- layer_out: bfloat16 [65536, 1024], P(('dp', 'ctx'))
- query_grad: bfloat16 [65536, 1024], P(('dp', 'ctx'))
- key_grad: bfloat16 [65536, 1024], P(('dp', 'ctx'))
- value_grad: bfloat16 [65536, 1024], P(('dp', 'ctx'))
- gate_grad: bfloat16 [65536, 1024], P(('dp', 'ctx'))
- gain_grad: float32 [1024], replicated
- weight_grad: float32 [1024, 1024], replicated
Inputs may be any that keep to these rules, and one draw needn't show every extreme that they name: Each row holds the lengths of the 4 users of one packed sequence, in order; they sum to 256, and the largest of each row is 128.
All inputs are finite; a program needn't handle non-finite values.
Results may differ from a plain program's by a relative error of at most 0.0059.
Values may be sent and summed in bfloat16 or wider, within the bound.
No kernel may reach another device: no remote copies, remote signals or barrier semaphores. Data moves between devices by JAX's collectives and lax.ppermute only.
A program may use at most 64 MiB of HBM per device.

v0:
```python
import jax
import jax.numpy as jnp
from jax import lax
from jax.sharding import PartitionSpec as P

HEADS = 4


def user_index(user_ends, positions):
    return jnp.sum(
        (positions[:, None] >= user_ends[None, :]).astype(jnp.int32), axis=1, dtype=jnp.int32
    )


def silu_slope(scores):
    sigma = jax.nn.sigmoid(scores)
    return sigma * (1.0 + scores * (1.0 - sigma))


def per_device(
    query_rows, key_rows, value_rows, gate_rows, lengths, norm_gain, out_weight, cotangent
):
    row_count, model_width = query_rows.shape
    head_count = HEADS
    head_size = model_width // head_count
    score_scale = head_size ** (-0.5)
    group_len = row_count * lax.axis_size("ctx")
    user_ends = jnp.cumsum(lengths[0])
    own_index = lax.axis_index("ctx") * row_count + jnp.arange(row_count, dtype=jnp.int32)
    own_user = user_index(user_ends, own_index)

    def split(array):
        return array.reshape(array.shape[0], head_count, head_size)

    def events_of(length):
        positions = jnp.arange(length, dtype=jnp.int32)
        return (positions, user_index(user_ends, positions))

    def allowed(query_index, query_user, key_index, key_user):
        return (query_user[:, None] == key_user[None, :]) & (
            key_index[None, :] <= query_index[:, None]
        )

    query_heads = split(query_rows)
    head_zeros = jnp.zeros((row_count, head_count, head_size), jnp.float32)
    key_part = lax.all_gather(key_rows, "ctx", axis=0, tiled=True)
    value_part = lax.all_gather(value_rows, "ctx", axis=0, tiled=True)
    key_index, key_user = events_of(key_part.shape[0])
    visible = allowed(own_index, own_user, key_index, key_user)

    def attend_work(accum_in):
        scores = (
            jnp.einsum(
                "qhd,khd->hqk", query_heads, split(key_part), preferred_element_type=jnp.float32
            )
            * score_scale
        )
        weights = jnp.where(visible[None], jax.nn.silu(scores), 0.0).astype(jnp.bfloat16)
        return jnp.einsum(
            "hqk,khd->qhd", weights, split(value_part), preferred_element_type=jnp.float32
        )

    attended = lax.cond(
        jnp.any(visible), attend_work, lambda accum_in: accum_in, head_zeros
    ).reshape(row_count, model_width)
    row_mean = jnp.mean(attended, axis=1, keepdims=True)
    centered = attended - row_mean
    row_var = jnp.mean(centered * centered, axis=1, keepdims=True)
    inv_std = lax.rsqrt(row_var + 1e-05)
    normed = centered * inv_std
    gated = (normed * norm_gain * gate_rows).astype(jnp.bfloat16)
    layer_out = jnp.dot(gated, out_weight, preferred_element_type=jnp.float32).astype(jnp.bfloat16)
    gated_grad = jnp.dot(cotangent, out_weight.T, preferred_element_type=jnp.float32)
    weight_part = jnp.dot(gated.T, cotangent, preferred_element_type=jnp.float32)
    gain_part = jnp.sum(gated_grad * gate_rows * normed, axis=0)
    gate_grad = (gated_grad * normed * norm_gain).astype(jnp.bfloat16)
    inner = gated_grad * gate_rows * norm_gain
    out_grad = (
        (
            inner
            - jnp.mean(inner, axis=1, keepdims=True)
            - normed * jnp.mean(inner * normed, axis=1, keepdims=True)
        )
        * inv_std
    ).astype(jnp.bfloat16)
    grad_heads = split(out_grad)
    group_zeros = jnp.zeros((group_len, head_count, head_size), jnp.float32)
    backward_key_part = lax.all_gather(key_rows, "ctx", axis=0, tiled=True)
    backward_value_part = lax.all_gather(value_rows, "ctx", axis=0, tiled=True)
    length = backward_key_part.shape[0]
    key_index, key_user = events_of(length)
    backward_visible = allowed(own_index, own_user, key_index, key_user)

    def backward_work(accum_in):
        part_keys = split(backward_key_part)
        scores = (
            jnp.einsum("qhd,khd->hqk", query_heads, part_keys, preferred_element_type=jnp.float32)
            * score_scale
        )
        weights = jnp.where(backward_visible[None], jax.nn.silu(scores), 0.0).astype(jnp.bfloat16)
        attn_grad = jnp.einsum(
            "qhd,khd->hqk",
            grad_heads,
            split(backward_value_part),
            preferred_element_type=jnp.float32,
        )
        score_grad = jnp.where(backward_visible[None], attn_grad * silu_slope(scores), 0.0).astype(
            jnp.bfloat16
        )
        query_acc = jnp.einsum(
            "hqk,khd->qhd", score_grad, part_keys, preferred_element_type=jnp.float32
        )
        key_piece = jnp.einsum(
            "hqk,qhd->khd", score_grad, query_heads, preferred_element_type=jnp.float32
        )
        value_piece = jnp.einsum(
            "hqk,qhd->khd", weights, grad_heads, preferred_element_type=jnp.float32
        )
        return (query_acc, key_piece, value_piece)

    query_sum, key_whole, value_whole = lax.cond(
        jnp.any(backward_visible),
        backward_work,
        lambda accum_in: accum_in,
        (head_zeros, group_zeros, group_zeros),
    )
    key_sum, value_sum = (
        lax.psum_scatter(key_whole, "ctx", scatter_dimension=0, tiled=True),
        lax.psum_scatter(value_whole, "ctx", scatter_dimension=0, tiled=True),
    )
    query_grad = (query_sum * score_scale).reshape(row_count, model_width).astype(jnp.bfloat16)
    key_grad = (key_sum * score_scale).reshape(row_count, model_width).astype(jnp.bfloat16)
    value_grad = value_sum.reshape(row_count, model_width).astype(jnp.bfloat16)
    weight_grad, gain_grad = lax.psum((weight_part, gain_part), ("dp", "ctx"))
    return (layer_out, query_grad, key_grad, value_grad, gate_grad, gain_grad, weight_grad)


def solution(mesh):
    placed = (
        P(("dp", "ctx"), None),
        P(("dp", "ctx"), None),
        P(("dp", "ctx"), None),
        P(("dp", "ctx"), None),
        P("dp", None),
        P(),
        P(),
        P(("dp", "ctx"), None),
    )
    return jax.shard_map(
        per_device,
        mesh=mesh,
        in_specs=placed,
        out_specs=(
            P(("dp", "ctx"), None),
            P(("dp", "ctx"), None),
            P(("dp", "ctx"), None),
            P(("dp", "ctx"), None),
            P(("dp", "ctx"), None),
            P(),
            P(),
        ),
        check_vma=False,
    )
```

profile of v0, /device:TPU:1, one launch (start us, length us, event | category | flops | bytes accessed | tf_op | source)
XLA Modules:
  0.0 338.1 jit_solution(5513484163062671362)
XLA Ops:
  8.1 1.0 reduce-window.8
  9.2 0.7 fusion.35
  10.6 1.1 copy.53
  11.7 8.9 %all_gather.8 = bf16[256,1024]{1,0:T(8,128)(2,1)S(1)} all-gather(bf16[128,1024]{1,0:T(8,128)(2,1)} %param.13), channel_id=1, replica_groups=mesh['dp'=256,'ctx'=2] {'ctx'}, dimensions={0}, use_global_device_ids=true | all-gather | bytes 786432 | tf_op jit(solution)/shard_map/all_gather | solution.py:46
  20.6 4.0 %all_gather.9 = bf16[256,1024]{1,0:T(8,128)(2,1)} all-gather(bf16[128,1024]{1,0:T(8,128)(2,1)} %param.14), channel_id=1, replica_groups=mesh['dp'=256,'ctx'=2] {'ctx'}, dimensions={0}, use_global_device_ids=true | all-gather | bytes 786432 | tf_op jit(solution)/shard_map/all_gather | solution.py:47
  24.7 1.5 conditional.2
  24.7 1.5 convolution_bitcast_fusion
  26.9 2.1 multiply_reduce_fusion
  29.0 1.1 multiply_convert_fusion
  30.1 4.4 %conditional.3 = (f32[128,4,256]{2,0,1:T(8,128)}, f32[256,4,256]{2,0,1:T(8,128)}, f32[256,4,256]{2,0,1:T(8,128)}) conditional(s32[]{:T(128)} %convert_element_type.57, () %tuple.24, (pred[128,256]{1,0:T(8,128)(4,1)S(1)}, bf16[128,1024]{1,0:T(8,128)(2,1)S(1)}, bf16[256,1024]{1,0:T(8,128)(2,1)S(1)}, bf16[256,1024]{1,0:T(8,128)(2,1)S(1)}, ...), branch_computations={%region_10.11_spmd, %region_11.12_spmd} | conditional | flops 337772544 | bytes 7667736 | solution.py:121
  30.8 1.0 convolution_bitcast_fusion.3
  31.8 1.4 convolution_bitcast_fusion.1
  33.2 1.3 convolution_bitcast_fusion.2
  35.5 2.7 fusion.37
  38.2 1.1 fusion.33
  39.3 0.7 copy.70
  40.0 101.4 %psum.14 = f32[1024]{0:T(1024)} all-reduce(f32[1024]{0:T(1024)S(1)} %get-tuple-element.62), channel_id=1, replica_groups=mesh['dp'=256,'ctx'=2] {'dp','ctx'}, use_global_device_ids=true, to_apply=%region_15.16 | all-reduce | flops 1024 | bytes 8192 | tf_op jit(solution)/shard_map/psum | solution.py:134
  141.5 1.1 convolution_convert_fusion
  142.6 1.1 fusion.34
  143.7 0.7 copy.71
  144.4 1.1 convert_bitcast_fusion
  145.5 0.7 copy.72
  146.2 179.6 %all-reduce.2.cloned.1.call-done = f32[1024,1024]{1,0:T(8,128)} async-done(((f32[1024,1024]{1,0:T(8,128)}), f32[1024,1024]{1,0:T(8,128)}) %all-reduce.2.cloned.1.call-update) | async-done | bytes 4194320 | tf_op jit(solution)/shard_map/psum | solution.py:134
  325.9 4.8 %copy.114 = f32[1024,1024]{1,0:T(8,128)} copy(f32[1024,1024]{1,0:T(8,128)} %all-reduce.2.cloned.1.call-done) | data formatting | bytes 8388608
  (29 shorter events, 2.5 us)
Async XLA Ops:
  8.0 18.6 %copy-start = (bf16[1024,1024]{1,0:T(8,128)(2,1)S(1)}, bf16[1024,1024]{1,0:T(8,128)(2,1)}, u32[]{:S(2)}) copy-start(bf16[1024,1024]{1,0:T(8,128)(2,1)} %param.18) | copy-start | bytes 6291460
  8.0 134.6 %reduce-scatter.3.cloned.1.call-start = ((), (), s32[]{:S(2)}) async-start(), calls=%async_computation.2 | async-start | bytes 1572864 | tf_op jit(solution)/shard_map/reduce_scatter | solution.py:128
  26.2 0.7 copy-start.4
  26.6 2.4 copy-start.1
  26.9 3.2 copy-start.3
  34.5 0.9 copy-start.2
  34.5 109.9 %reduce-scatter.5.cloned.1.call-start = ((), (), s32[]{:S(2)}) async-start(), calls=%async_computation.3 | async-start | bytes 1572864 | tf_op jit(solution)/shard_map/reduce_scatter | solution.py:129
  35.3 290.6 %all-reduce.2.cloned.1.call-start = ((), (), s32[]{:S(2)}) async-start(), calls=%async_computation.4 | async-start | bytes 8388608 | tf_op jit(solution)/shard_map/psum | solution.py:134
Sparse Core Ops, SparseCore 0:
  34.7 16.8 reduce-scatter.2
  54.6 17.9 reduce-scatter.4
Sparse Core Ops, SparseCore 1:
  41.3 284.5 all-reduce.1
where the time goes:
time: 340 us; the launch traced here: 338 us
  waiting for transfers between devices  180 us (53%)
  blocking collectives  114 us (34%)
  between operations  16.2 us (5%)
  matrix products  11.9 us (4%)
  local copies, waits for them, and re-layouts  8.55 us (3%)
  other arithmetic  6.51 us (2%)
    psum x1, waiting for transfers between devices, per_device(): weight_grad, gain_grad = lax.psum((weight_part, gain_part), ('dp', 'ctx'))  180 us
    psum x1, blocking collectives, per_device(): weight_grad, gain_grad = lax.psum((weight_part, gain_part), ('dp', 'ctx'))  101 us
    all_gather x1, blocking collectives, per_device(): key_part = lax.all_gather(key_rows, 'ctx', axis=0, tiled=True)  8.9 us
  transfers between devices with their start and end apart: 3, of which 1 were waited for; matrix products, arithmetic and copies ran while one was open for 3% of the time, Pallas kernels for 0%

commit v1 on v0

v1 whole, which is shorter than its diff:
```python
import functools

import jax
import jax.numpy as jnp
from jax import lax
from jax.experimental import pallas as pl
from jax.experimental.pallas import tpu as pltpu
from jax.sharding import Mesh, PartitionSpec as P

HEADS = 4
HEAD_DIM = 256
WIDTH = 1024
ROWS = 128
GROUP = 256
PLANE = ("z", "y")
CHIPS = ("z", "y", "x")
DEVICES = ("z", "y", "x", "c")
F32 = jnp.float32
BF16 = jnp.bfloat16
VMEM = pl.BlockSpec(memory_space=pltpu.VMEM)
SMEM = pl.BlockSpec(memory_space=pltpu.SMEM)
PARAMS = pltpu.CompilerParams(vmem_limit_bytes=48 * 1024 * 1024)


def dot(a, b, contract):
    return lax.dot_general(a, b, (contract, ((), ())), preferred_element_type=F32)


def visible_mask(core, lengths):
    def place(shape, axis):
        local = lax.broadcasted_iota(jnp.int32, shape, axis)
        return jnp.where(local < ROWS, core * ROWS + local, (1 - core) * ROWS + local - ROWS)

    row, column = place((GROUP, 1), 0), place((GROUP, GROUP), 1)
    start = jnp.zeros((GROUP, 1), jnp.int32)
    end = 0
    for user in range(3):
        end = end + lengths[0, user]
        start = jnp.where(row >= end, end, start)
    return (column <= row) & (column >= start)


def both(own, other, item, columns):
    rows = slice(item * ROWS, (item + 1) * ROWS)
    return jnp.concatenate([own[rows, columns], other[rows, columns]], axis=0)


def head_columns(head):
    return slice(head * HEAD_DIM, (head + 1) * HEAD_DIM)


def forward_kernel(core_ref, lengths, own, other, gain, part, normed, inv_std, gated_own, attended, gated):
    core = core_ref[0]
    visible = visible_mask(core, lengths)
    for head in range(HEADS):
        columns = head_columns(head)
        scores = dot(both(own, other, 0, columns), both(own, other, 1, columns), ((1,), (1,))) * (HEAD_DIM**-0.5)
        weights = jnp.where(visible, scores * jax.nn.sigmoid(scores), 0.0).astype(BF16)
        attended[:, columns] = dot(weights, both(own, other, 2, columns), ((1,), (0,)))
    chunk = 32
    for first in range(0, GROUP, chunk):
        rows = slice(first, first + chunk)
        values = attended[rows, :]
        centered = values - jnp.mean(values, axis=1, keepdims=True)
        inverse = lax.rsqrt(jnp.mean(centered * centered, axis=1, keepdims=True) + 1e-05)
        unit = centered * inverse
        normed[rows, :] = unit
        inv_std[rows, :] = inverse
        source, at = (own, first) if first < ROWS else (other, first - ROWS)
        gate = source[3 * ROWS + at : 3 * ROWS + at + chunk, :].astype(F32)
        result = (unit * gain[...] * gate).astype(BF16)
        gated[0, rows, :] = result[:, : WIDTH // 2]
        gated[1, rows, :] = result[:, WIDTH // 2 :]
        if first < ROWS:
            gated_own[rows, :] = result
    for x in range(4):
        mine = gated[core, :, x * 128 : (x + 1) * 128]
        for half in range(2):
            wide = slice(half * 512, (half + 1) * 512)
            block = dot(mine, both(own, other, 4, wide), ((0,), (0,))).astype(BF16)
            for i in range(8):
                for j in range(4):
                    part[x, i * 8 + half * 4 + j] = block[i * 16 : (i + 1) * 16, j * 128 : (j + 1) * 128]


def backward_kernel(
    core_ref, lengths, own, other, gain, normed, inv_std, gated_own, weight,
    layer_out, query_grad, key_grad, value_grad, gate_grad, gated_grad, out_grad,
):
    core = core_ref[0]
    visible = visible_mask(core, lengths)
    scale = HEAD_DIM**-0.5
    gated_grad[...] = dot(both(own, other, 4, slice(None)), weight[...], ((1,), (1,)))
    layer_out[...] = dot(gated_own[...], weight[...], ((1,), (0,))).astype(BF16)
    chunk = 32
    for first in range(0, GROUP, chunk):
        rows = slice(first, first + chunk)
        unit = normed[rows, :]
        source, at = (own, first) if first < ROWS else (other, first - ROWS)
        gate = source[3 * ROWS + at : 3 * ROWS + at + chunk, :].astype(F32)
        scaled = gated_grad[rows, :] * gain[...]
        if first < ROWS:
            gate_grad[rows, :] = (scaled * unit).astype(BF16)
        inner = scaled * gate
        inner = (
            inner
            - jnp.mean(inner, axis=1, keepdims=True)
            - unit * jnp.mean(inner * unit, axis=1, keepdims=True)
        ) * inv_std[rows, :]
        out_grad[rows, :] = inner.astype(BF16)
    for head in range(HEADS):
        columns = head_columns(head)
        queries, keys = both(own, other, 0, columns), both(own, other, 1, columns)
        values, grads = both(own, other, 2, columns), out_grad[:, columns]
        scores = dot(queries, keys, ((1,), (1,))) * scale
        sigma = jax.nn.sigmoid(scores)
        weights = jnp.where(visible, scores * sigma, 0.0).astype(BF16)
        slope = sigma * (1.0 + scores * (1.0 - sigma))
        score_grad = jnp.where(visible, dot(grads, values, ((1,), (1,))) * slope, 0.0).astype(BF16)
        query_grad[:, columns] = (dot(score_grad[:ROWS, :], keys, ((1,), (0,))) * scale).astype(BF16)
        key_grad[:, columns] = (dot(score_grad[:, :ROWS], queries, ((0,), (0,))) * scale).astype(BF16)
        value_grad[:, columns] = dot(weights[:, :ROWS], grads, ((0,), (0,))).astype(BF16)


def finish_kernel(core_ref, mine, other, weight, gain, weight_grad, gain_grad):
    def write(source):
        total = jnp.zeros((ROWS, 128), F32)
        for j in range(8):
            columns = slice(j * 128, (j + 1) * 128)
            block = jnp.concatenate([source[0, i * 8 + j].astype(F32) for i in range(8)], axis=0)
            weight_grad[:, columns] = block
            total = total + block * weight[:, columns].astype(F32)
        gain_grad[...] = jnp.sum(total.T, axis=0, keepdims=True) / gain[...]

    step = pl.program_id(0)

    @pl.when(step < 4)
    def _():
        write(mine)

    @pl.when(step >= 4)
    def _():
        write(other)


def per_device(query_rows, key_rows, value_rows, gate_rows, lengths, norm_gain, out_weight, cotangent):
    core = lax.axis_index("c").astype(jnp.int32).reshape(1)
    gain = norm_gain.reshape(1, WIDTH)
    swap = [(0, 1), (1, 0)]
    own = jnp.concatenate([query_rows, key_rows, value_rows, gate_rows, cotangent], axis=0)
    other = lax.ppermute(own, "c", swap)
    shape = jax.ShapeDtypeStruct
    part, normed, inv_std, gated_own = pl.pallas_call(
        forward_kernel,
        out_shape=[
            shape((4, 64, 16, 128), BF16),
            shape((GROUP, WIDTH), F32),
            shape((GROUP, 1), F32),
            shape((ROWS, WIDTH), BF16),
        ],
        in_specs=[SMEM, SMEM, VMEM, VMEM, VMEM],
        out_specs=[VMEM] * 4,
        scratch_shapes=[pltpu.VMEM((GROUP, WIDTH), F32), pltpu.VMEM((2, GROUP, WIDTH // 2), BF16)],
        compiler_params=PARAMS,
        cost_estimate=pl.CostEstimate(flops=540_000_000, bytes_accessed=6_000_000, transcendentals=300_000),
        name="forward",
    )(core, lengths, own, other, gain)

    pieces = lax.all_to_all(part, "x", 0, 0, tiled=True)

    layer_out, query_grad, key_grad, value_grad, gate_grad = pl.pallas_call(
        backward_kernel,
        out_shape=[shape((ROWS, WIDTH), BF16)] * 5,
        in_specs=[SMEM, SMEM] + [VMEM] * 7,
        out_specs=[VMEM] * 5,
        scratch_shapes=[pltpu.VMEM((GROUP, WIDTH), F32), pltpu.VMEM((GROUP, WIDTH), BF16)],
        compiler_params=PARAMS,
        cost_estimate=pl.CostEstimate(flops=1_800_000_000, bytes_accessed=9_000_000, transcendentals=300_000),
        name="backward",
    )(core, lengths, own, other, gain, normed, inv_std, gated_own, out_weight)

    block = jnp.sum(pieces.astype(F32), axis=0).astype(BF16)
    pieces = lax.all_to_all(block, PLANE, 0, 0, tiled=True)
    total = jnp.sum(pieces.astype(F32), axis=0).astype(BF16)
    block = lax.all_to_all(jnp.broadcast_to(total[None], (64, 16, 128)), PLANE, 0, 0, tiled=True)
    mine = lax.all_to_all(jnp.broadcast_to(block[None], (4, 64, 16, 128)), "x", 0, 0, tiled=True)
    theirs = lax.ppermute(mine, "c", swap)

    def target(step, core):
        return jnp.where(step < 4, core[0], 1 - core[0]) * 4 + step % 4

    weight_grad, gain_grad = pl.pallas_call(
        finish_kernel,
        out_shape=[shape((WIDTH, WIDTH), F32), shape((1, WIDTH), F32)],
        grid_spec=pltpu.PrefetchScalarGridSpec(
            num_scalar_prefetch=1,
            grid=(8,),
            in_specs=[
                pl.BlockSpec((1, 64, 16, 128), lambda s, core: (jnp.minimum(s, 3), 0, 0, 0)),
                pl.BlockSpec((1, 64, 16, 128), lambda s, core: (jnp.maximum(s - 4, 0), 0, 0, 0)),
                pl.BlockSpec((ROWS, WIDTH), lambda s, core: (target(s, core), 0)),
                pl.BlockSpec((1, 128), lambda s, core: (0, target(s, core))),
            ],
            out_specs=[
                pl.BlockSpec((ROWS, WIDTH), lambda s, core: (target(s, core), 0)),
                pl.BlockSpec((1, 128), lambda s, core: (0, target(s, core))),
            ],
        ),
        compiler_params=PARAMS,
        cost_estimate=pl.CostEstimate(flops=3_000_000, bytes_accessed=8_000_000, transcendentals=0),
        name="finish",
    )(core, mine, theirs, out_weight, gain)
    return (layer_out, query_grad, key_grad, value_grad, gate_grad, gain_grad.reshape(WIDTH), weight_grad)


def solution(mesh):
    chips = Mesh(mesh.devices.reshape(8, 8, 4, 2), DEVICES)
    rows = P(DEVICES, None)
    return jax.shard_map(
        per_device,
        mesh=chips,
        in_specs=(rows, rows, rows, rows, P(CHIPS, None), P(), P(), rows),
        out_specs=(rows, rows, rows, rows, rows, P(), P()),
        check_vma=False,
    )
```

time: 340 us -> 107 us (0.31)
  waiting for transfers between devices: 180 us -> 2.64 us
  blocking collectives: 114 us -> 71.2 us
  starting transfers between devices: 0.12 us -> 16 us
  between operations: 16.2 us -> 0.79 us
  matrix products: 11.9 us -> 0 us
  Pallas kernels: 0 us -> 10.2 us
  other arithmetic: 6.51 us -> 1.54 us
  local copies, waits for them, and re-layouts: 8.55 us -> 4.16 us
    psum x1 -> x0, waiting for transfers between devices: 180 us -> none  [per_device(): weight_grad, gain_grad = lax.psum((weight_part, gain_part), ('dp', 'ctx'))]
    psum x1 -> x0, blocking collectives: 101 us -> none  [per_device(): weight_grad, gain_grad = lax.psum((weight_part, gain_part), ('dp', 'ctx'))]
    all_to_all x0 -> x4, blocking collectives: none -> 71.2 us  [the longest x1 23.4 us: per_device(): pieces = lax.all_to_all(block, PLANE, 0, 0, tiled=True)]
    ppermute x0 -> x2, starting transfers between devices: none -> 16 us  [the longest x1 8.79 us: per_device(): other = lax.ppermute(own, 'c', swap)]
    all_gather x2 -> x0, blocking collectives: 12.9 us -> none  [the longest x1 8.9 us: per_device(): key_part = lax.all_gather(key_rows, 'ctx', axis=0, tiled=True)]
    dot_general x9 -> x0, matrix products: 11.9 us -> none  [the longest x1 2.75 us: per_device(): jnp.dot(gated.T, cotangent, preferred_element_type=jnp.float32)]
    pallas_call x0 -> x3, Pallas kernels: none -> 10.2 us  [the longest x1 4.07 us: per_device(): pl.pallas_call(backward_kernel, out_shape=[shape((ROWS, WIDTH), BF16)] *...]
  transfers between devices with their start and end apart: 3 -> 2, of which waited for: 1 -> 1; matrix products, arithmetic and copies ran while one was open for 3% -> 0% of each run, Pallas kernels for 0% -> 4%
where the time goes in v1:
time: 107 us
  blocking collectives  71.2 us (67%)
  starting transfers between devices  16 us (15%)
  Pallas kernels  10.2 us (10%)
  local copies, waits for them, and re-layouts  4.16 us (4%)
  waiting for transfers between devices  2.64 us (2%)
  other arithmetic  1.54 us (1%)
    all_to_all x1, blocking collectives, per_device(): pieces = lax.all_to_all(block, PLANE, 0, 0, tiled=True)  23.4 us
    all_to_all x1, blocking collectives, per_device(): pieces = lax.all_to_all(part, 'x', 0, 0, tiled=True)  18 us
    all_to_all x1, blocking collectives, per_device(): lax.all_to_all(jnp.broadcast_to(total[None], (64, 16, 128)), PLANE, 0, 0,...  16.4 us
    all_to_all x1, blocking collectives, per_device(): lax.all_to_all(jnp.broadcast_to(block[None], (4, 64, 16, 128)), 'x', 0, 0...  13.4 us
    ppermute x1, starting transfers between devices, per_device(): other = lax.ppermute(own, 'c', swap)  8.79 us
    ppermute x1, starting transfers between devices, per_device(): theirs = lax.ppermute(mine, 'c', swap)  7.26 us
    pallas_call x1, Pallas kernels, per_device(): pl.pallas_call(backward_kernel, out_shape=[shape((ROWS, WIDTH), BF16)] *...  4.07 us
    unnamed x18, local copies, waits for them, and re-layouts  3.97 us
  transfers between devices with their start and end apart: 2, of which 1 were waited for; matrix products, arithmetic and copies ran while one was open for 0% of the time, Pallas kernels for 4%

profile of v1, /device:TPU:1, one launch (start us, length us, event | category | flops | bytes accessed | tf_op | source)
XLA Modules:
  0.0 106.6 jit_solution(2004880762007804886)
XLA Ops:
  0.6 0.0 copy-start.5
  0.6 0.0 copy-start.6
  0.7 0.0 copy-start.2
  0.7 1.0 constant_dynamic-update-slice_fusion.4
  1.7 1.0 constant_dynamic-update-slice_fusion.3
  2.7 1.0 constant_dynamic-update-slice_fusion.2
  3.6 0.0 copy-done.5
  3.7 8.8 %collective-permute-start = (bf16[640,1024]{1,0:T(8,128)(2,1)S(1)}, bf16[640,1024]{1,0:T(8,128)(2,1)S(1)}, u32[]{:S(2)}, u32[]{:S(2)}) collective-permute-start(bf16[640,1024]{1,0:T(8,128)(2,1)S(1)} %constant_dynamic-update-slice_fusion.own), channel_id=1, source_target_pairs={{0,1},{1,0},{2,3},{3,2},{4,5},{5,4},{6,7},{7,6},{8,9},{9,8},{10,11... | collective-permute-start | bytes 3932168 | tf_op jit(solution)/shard_map/ppermute | solution.py:151
  12.5 2.6 %collective-permute-done.other = bf16[640,1024]{1,0:T(8,128)(2,1)S(1)} collective-permute-done((bf16[640,1024]{1,0:T(8,128)(2,1)S(1)}, bf16[640,1024]{1,0:T(8,128)(2,1)S(1)}, u32[]{:S(2)}, u32[]{:S(2)}) %collective-permute-start) | collective-permute-done | bytes 1310752 | tf_op jit(solution)/shard_map/ppermute | solution.py:151
  15.2 2.2 %forward.1 = (bf16[4,64,16,128]{3,2,1,0:T(8,128)(2,1)S(1)}, f32[256,1024]{1,0:T(8,128)S(1)}, f32[256,1]{1,0:T(8,128)S(1)}, bf16[128,1024]{1,0:T(8,128)(2,1)S(1)}) custom-call(s32[1]{0:T(128)} %bitcast.core_ref, s32[1,4]{1,0:T(1,128)S(1)} %copy-done.2, bf16[640,1024]{1,0:T(8,128)(2,1)S(1)} %constant_dynamic-update-slice_fusion.own, ...), custom_call_target="tpu_custom_call" | custom-call | flops 540000000 | bytes 6000000 | tf_op jit(solution)/shard_map/forward/pallas_call | solution.py:153
  17.3 0.0 copy-start.3
  17.3 1.0 copy-done.3
  18.3 18.0 %all_to_all.20 = bf16[4,64,16,128]{3,2,1,0:T(8,128)(2,1)} all-to-all(bf16[4,64,16,128]{3,2,1,0:T(8,128)(2,1)S(1)} %get-tuple-element.26), channel_id=1, replica_groups=mesh['z'=8,'y'=8,'x'=4,'c'=2] {'x'}, dimensions={0} | all-to-all | bytes 2097152 | tf_op jit(solution)/shard_map/all_to_all | solution.py:169
  36.3 1.5 %reduce_sum.24 = bf16[64,16,128]{2,1,0:T(8,128)(2,1)S(1)} reduce(bf16[4,64,16,128]{3,2,1,0:T(8,128)(2,1)} %all_to_all.20, bf16[]{:T(256)} %constant.7.clone.1), dimensions={0}, to_apply=%region_0.0 | reduce | flops 393216 | bytes 1310722 | tf_op jit(solution)/shard_map/reduce_sum | solution.py:182
  37.7 23.4 %all_to_all.21 = bf16[64,16,128]{2,1,0:T(8,128)(2,1)S(1)} all-to-all(bf16[64,16,128]{2,1,0:T(8,128)(2,1)S(1)} %reduce_sum.24), channel_id=1, replica_groups=mesh['z'=8,'y'=8,'x'=4,'c'=2] {'z','y'}, dimensions={0} | all-to-all | bytes 524288 | tf_op jit(solution)/shard_map/all_to_all | solution.py:183
  61.2 0.1 reduce_sum.25
  61.3 16.4 %all_to_all.22 = bf16[64,16,128]{2,1,0:T(8,128)(2,1)S(1)} all-to-all(bf16[64,16,128]{2,1,0:T(8,128)(2,1)S(1)} %broadcast_in_dim.4), channel_id=1, replica_groups=mesh['z'=8,'y'=8,'x'=4,'c'=2] {'z','y'}, dimensions={0} | all-to-all | bytes 524288 | tf_op jit(solution)/shard_map/all_to_all | solution.py:185
  77.7 0.1 broadcast_in_dim.5
  77.9 0.0 copy-start
  77.9 13.4 %all_to_all.23.mine = bf16[4,64,16,128]{3,2,1,0:T(8,128)(2,1)S(1)} all-to-all(bf16[4,64,16,128]{3,2,1,0:T(8,128)(2,1)S(1)} %broadcast_in_dim.5), channel_id=1, replica_groups=mesh['z'=8,'y'=8,'x'=4,'c'=2] {'x'}, dimensions={0} | all-to-all | bytes 2097152 | tf_op jit(solution)/shard_map/all_to_all | solution.py:186
  91.3 7.3 %collective-permute-start.1 = (bf16[4,64,16,128]{3,2,1,0:T(8,128)(2,1)S(1)}, bf16[4,64,16,128]{3,2,1,0:T(8,128)(2,1)S(1)}, u32[]{:S(2)}, u32[]{:S(2)}) collective-permute-start(bf16[4,64,16,128]{3,2,1,0:T(8,128)(2,1)S(1)} %all_to_all.23.mine), channel_id=1, source_target_pairs={{0,1},{1,0},{2,3},{3,2},{4,5},{5,4},{6,7},{7,6},{8,9},{9,8},{10,11... | collective-permute-start | bytes 3145736 | tf_op jit(solution)/shard_map/ppermute | solution.py:187
  98.6 4.1 %backward.1 = (bf16[128,1024]{1,0:T(8,128)(2,1)}, bf16[128,1024]{1,0:T(8,128)(2,1)}, bf16[128,1024]{1,0:T(8,128)(2,1)}, bf16[128,1024]{1,0:T(8,128)(2,1)}, bf16[128,1024]{1,0:T(8,128)(2,1)}) custom-call(s32[1]{0:T(128)} %bitcast.core_ref, s32[1,4]{1,0:T(1,128)S(1)} %copy-done.2, bf16[640,1024]{1,0:T(8,128)(2,1)S(1)} %constant_dynamic-update-slice_fusion.own, ...), custom_call_target="tpu_custom_call" | custom-call | flops 1800000000 | bytes 9000000 | tf_op jit(solution)/shard_map/backward/pallas_call | solution.py:171
  102.6 0.0 collective-permute-done.1.other
  102.6 4.0 %finish.1 = (f32[1024,1024]{1,0:T(8,128)}, f32[1,1024]{1,0:T(1,128)}) custom-call(s32[1]{0:T(128)} %bitcast.core_ref, bf16[4,64,16,128]{3,2,1,0:T(8,128)(2,1)S(1)} %all_to_all.23.mine, bf16[4,64,16,128]{3,2,1,0:T(8,128)(2,1)S(1)} %collective-permute-done.1.other, bf16[1024,1024]{1,0:T(8,128)(2,1)S(1)} %copy-done, f32[1,1024]{1,0:T(1,128)S(1)} %bitcast.5), custom_call_target="tpu_custom_call" | custom-call | flops 3000000 | bytes 8000000 | tf_op jit(solution)/shard_map/finish/pallas_call | solution.py:192
  (10 shorter events, 0.1 us)
Async XLA Ops:
  0.6 3.0 %copy-start.5 = (bf16[128,1024]{1,0:T(8,128)(2,1)S(1)}, bf16[128,1024]{1,0:T(8,128)(2,1)}, u32[]{:S(2)}) copy-start(bf16[128,1024]{1,0:T(8,128)(2,1)} %param.11) | copy-start | bytes 786436
  0.6 3.0 %copy-start.6 = (bf16[128,1024]{1,0:T(8,128)(2,1)S(1)}, bf16[128,1024]{1,0:T(8,128)(2,1)}, u32[]{:S(2)}) copy-start(bf16[128,1024]{1,0:T(8,128)(2,1)} %param.15) | copy-start | bytes 786436
  0.7 14.5 %copy-start.2 = (s32[1,4]{1,0:T(1,128)S(1)}, s32[1,4]{1,0:T(1,128)}, u32[]{:S(2)}) copy-start(s32[1,4]{1,0:T(1,128)} %lengths.3) | copy-start | bytes 52
  0.7 14.5 %copy-start.1 = (f32[1024]{0:T(1024)S(1)}, f32[1024]{0:T(1024)}, u32[]{:S(2)}) copy-start(f32[1024]{0:T(1024)} %param.13) | copy-start | bytes 12292
  3.7 11.4 %collective-permute-start = (bf16[640,1024]{1,0:T(8,128)(2,1)S(1)}, bf16[640,1024]{1,0:T(8,128)(2,1)S(1)}, u32[]{:S(2)}, u32[]{:S(2)}) collective-permute-start(bf16[640,1024]{1,0:T(8,128)(2,1)S(1)} %constant_dynamic-update-slice_fusion.own), channel_id=1, source_target_pairs={{0,1},{1,0},{2,3},{3,2},{4,5},{5,4},{6,7},{7,6},{8,9},{9,8},{10,11... | collective-permute-start | bytes 3932168 | tf_op jit(solution)/shard_map/ppermute | solution.py:151
  17.3 1.0 copy-start.3
  77.7 20.8 %copy-start.4 = (f32[256,1024]{1,0:T(8,128)S(1)}, f32[256,1024]{1,0:T(8,128)}, u32[]{:S(2)}) copy-start(f32[256,1024]{1,0:T(8,128)} %copy-done.3) | copy-start | bytes 3145732
  77.9 20.7 %copy-start = (bf16[1024,1024]{1,0:T(8,128)(2,1)S(1)}, bf16[1024,1024]{1,0:T(8,128)(2,1)}, u32[]{:S(2)}) copy-start(bf16[1024,1024]{1,0:T(8,128)(2,1)} %weight.3) | copy-start | bytes 6291460
  91.3 11.4 %collective-permute-start.1 = (bf16[4,64,16,128]{3,2,1,0:T(8,128)(2,1)S(1)}, bf16[4,64,16,128]{3,2,1,0:T(8,128)(2,1)S(1)}, u32[]{:S(2)}, u32[]{:S(2)}) collective-permute-start(bf16[4,64,16,128]{3,2,1,0:T(8,128)(2,1)S(1)} %all_to_all.23.mine), channel_id=1, source_target_pairs={{0,1},{1,0},{2,3},{3,2},{4,5},{5,4},{6,7},{7,6},{8,9},{9,8},{10,11... | collective-permute-start | bytes 3145736 | tf_op jit(solution)/shard_map/ppermute | solution.py:187

commit v2 on v1

--- a/solution.py
+++ b/solution.py
@@ -19,7 +19,7 @@
 BF16 = jnp.bfloat16
 VMEM = pl.BlockSpec(memory_space=pltpu.VMEM)
 SMEM = pl.BlockSpec(memory_space=pltpu.SMEM)
-PARAMS = pltpu.CompilerParams(vmem_limit_bytes=48 * 1024 * 1024)
+PARAMS = pltpu.CompilerParams(vmem_limit_bytes=20 * 1024 * 1024)
 
 
 def dot(a, b, contract):
@@ -49,8 +49,12 @@
     return slice(head * HEAD_DIM, (head + 1) * HEAD_DIM)
 
 
-def forward_kernel(core_ref, lengths, own, other, gain, part, normed, inv_std, gated_own, attended, gated):
-    core = core_ref[0]
+def tile(index):
+    return slice(index * 16, (index + 1) * 16)
+
+
+def forward_kernel(lengths, own, other, gain, part, normed, inv_std, gated_own, attended, gated):
+    core = lax.axis_index("c")
     visible = visible_mask(core, lengths)
     for head in range(HEADS):
         columns = head_columns(head)
@@ -80,14 +84,14 @@
             block = dot(mine, both(own, other, 4, wide), ((0,), (0,))).astype(BF16)
             for i in range(8):
                 for j in range(4):
-                    part[x, i * 8 + half * 4 + j] = block[i * 16 : (i + 1) * 16, j * 128 : (j + 1) * 128]
+                    part[x, tile(i * 8 + half * 4 + j), :] = block[i * 16 : (i + 1) * 16, j * 128 : (j + 1) * 128]
 
 
 def backward_kernel(
-    core_ref, lengths, own, other, gain, normed, inv_std, gated_own, weight,
+    lengths, own, other, gain, normed, inv_std, gated_own, weight,
     layer_out, query_grad, key_grad, value_grad, gate_grad, gated_grad, out_grad,
 ):
-    core = core_ref[0]
+    core = lax.axis_index("c")
     visible = visible_mask(core, lengths)
     scale = HEAD_DIM**-0.5
     gated_grad[...] = dot(both(own, other, 4, slice(None)), weight[...], ((1,), (1,)))
@@ -122,94 +126,113 @@
         value_grad[:, columns] = dot(weights[:, :ROWS], grads, ((0,), (0,))).astype(BF16)
 
 
-def finish_kernel(core_ref, mine, other, weight, gain, weight_grad, gain_grad):
-    def write(source):
-        total = jnp.zeros((ROWS, 128), F32)
-        for j in range(8):
-            columns = slice(j * 128, (j + 1) * 128)
-            block = jnp.concatenate([source[0, i * 8 + j].astype(F32) for i in range(8)], axis=0)
-            weight_grad[:, columns] = block
-            total = total + block * weight[:, columns].astype(F32)
-        gain_grad[...] = jnp.sum(total.T, axis=0, keepdims=True) / gain[...]
-
-    step = pl.program_id(0)
-
-    @pl.when(step < 4)
-    def _():
-        write(mine)
-
-    @pl.when(step >= 4)
-    def _():
-        write(other)
+def chip_sum_kernel(pieces, total):
+    for first in range(0, 1024, 128):
+        rows = slice(first, first + 128)
+        value = pieces[0, rows, :].astype(F32) + pieces[1, rows, :].astype(F32)
+        total[rows, :] = (value + (pieces[2, rows, :].astype(F32) + pieces[3, rows, :].astype(F32))).astype(BF16)
+
+
+def plane_sum_kernel(pieces, total):
+    sums = [pieces[i].astype(F32) for i in range(4)]
+    for first in range(4, 64, 4):
+        sums = [sums[i] + pieces[first + i].astype(F32) for i in range(4)]
+    value = ((sums[0] + sums[1]) + (sums[2] + sums[3])).astype(BF16)
+    for i in range(64):
+        total[i] = value
+
+
+def finish_kernel(source, weight, gain, *rest):
+    weight_grad, gain_grad = rest[-2:]
+    total = jnp.zeros((ROWS, 128), F32)
+    for j in range(8):
+        columns = slice(j * 128, (j + 1) * 128)
+        block = jnp.concatenate([source[0, tile(i * 8 + j), :].astype(F32) for i in range(8)], axis=0)
+        weight_grad[:, columns] = block
+        total = total + block * weight[:, columns].astype(F32)
+    gain_grad[...] = jnp.sum(total.T, axis=0, keepdims=True) / gain[...]
+
+
+def finish(theirs, source, weight, gain, partial):
+    shape = jax.ShapeDtypeStruct
+
+    def place(step):
+        core = lax.axis_index("c")
+        return (1 - core if theirs else core) * 4 + step
+
+    row_block = pl.BlockSpec((ROWS, WIDTH), lambda s: (place(s), 0))
+    gain_block = pl.BlockSpec((1, 128), lambda s: (0, place(s)))
+    return pl.pallas_call(
+        finish_kernel,
+        out_shape=[shape((WIDTH, WIDTH), F32), shape((1, WIDTH), F32)],
+        grid=(4,),
+        in_specs=[pl.BlockSpec((1, 1024, 128), lambda s: (s, 0, 0)), row_block, gain_block]
+        + [pl.BlockSpec(memory_space=pl.ANY)] * len(partial),
+        out_specs=[row_block, gain_block],
+        input_output_aliases={3: 0, 4: 1} if partial else {},
+        compiler_params=PARAMS,
+        cost_estimate=pl.CostEstimate(flops=1_500_000, bytes_accessed=4_000_000, transcendentals=0),
+        name="finish_theirs" if partial else "finish_mine",
+    )(source, weight, gain, *partial)
 
 
 def per_device(query_rows, key_rows, value_rows, gate_rows, lengths, norm_gain, out_weight, cotangent):
-    core = lax.axis_index("c").astype(jnp.int32).reshape(1)
     gain = norm_gain.reshape(1, WIDTH)
     swap = [(0, 1), (1, 0)]
+    shape = jax.ShapeDtypeStruct
     own = jnp.concatenate([query_rows, key_rows, value_rows, gate_rows, cotangent], axis=0)
     other = lax.ppermute(own, "c", swap)
-    shape = jax.ShapeDtypeStruct
     part, normed, inv_std, gated_own = pl.pallas_call(
         forward_kernel,
         out_shape=[
-            shape((4, 64, 16, 128), BF16),
+            shape((4, 1024, 128), BF16),
             shape((GROUP, WIDTH), F32),
             shape((GROUP, 1), F32),
             shape((ROWS, WIDTH), BF16),
         ],
-        in_specs=[SMEM, SMEM, VMEM, VMEM, VMEM],
+        in_specs=[SMEM, VMEM, VMEM, VMEM],
         out_specs=[VMEM] * 4,
         scratch_shapes=[pltpu.VMEM((GROUP, WIDTH), F32), pltpu.VMEM((2, GROUP, WIDTH // 2), BF16)],
         compiler_params=PARAMS,
         cost_estimate=pl.CostEstimate(flops=540_000_000, bytes_accessed=6_000_000, transcendentals=300_000),
         name="forward",
-    )(core, lengths, own, other, gain)
+    )(lengths, own, other, gain)
 
     pieces = lax.all_to_all(part, "x", 0, 0, tiled=True)
 
     layer_out, query_grad, key_grad, value_grad, gate_grad = pl.pallas_call(
         backward_kernel,
         out_shape=[shape((ROWS, WIDTH), BF16)] * 5,
-        in_specs=[SMEM, SMEM] + [VMEM] * 7,
+        in_specs=[SMEM] + [VMEM] * 7,
         out_specs=[VMEM] * 5,
         scratch_shapes=[pltpu.VMEM((GROUP, WIDTH), F32), pltpu.VMEM((GROUP, WIDTH), BF16)],
         compiler_params=PARAMS,
         cost_estimate=pl.CostEstimate(flops=1_800_000_000, bytes_accessed=9_000_000, transcendentals=300_000),
         name="backward",
-    )(core, lengths, own, other, gain, normed, inv_std, gated_own, out_weight)
-
-    block = jnp.sum(pieces.astype(F32), axis=0).astype(BF16)
-    pieces = lax.all_to_all(block, PLANE, 0, 0, tiled=True)
-    total = jnp.sum(pieces.astype(F32), axis=0).astype(BF16)
-    block = lax.all_to_all(jnp.broadcast_to(total[None], (64, 16, 128)), PLANE, 0, 0, tiled=True)
-    mine = lax.all_to_all(jnp.broadcast_to(block[None], (4, 64, 16, 128)), "x", 0, 0, tiled=True)
+    )(lengths, own, other, gain, normed, inv_std, gated_own, out_weight)
+
+    block = pl.pallas_call(
+        chip_sum_kernel,
+        out_shape=shape((1024, 128), BF16),
+        in_specs=[VMEM],
+        out_specs=VMEM,
+        compiler_params=PARAMS,
+        name="chip_sum",
+    )(pieces)
+    pieces = lax.all_to_all(block.reshape(64, 16, 128), PLANE, 0, 0, tiled=True)
+    total = pl.pallas_call(
+        plane_sum_kernel,
+        out_shape=shape((64, 16, 128), BF16),
+        in_specs=[VMEM],
+        out_specs=VMEM,
+        compiler_params=PARAMS,
+        name="plane_sum",
+    )(pieces)
+    block = lax.all_to_all(total, PLANE, 0, 0, tiled=True).reshape(1, 1024, 128)
+    mine = lax.all_to_all(jnp.broadcast_to(block, (4, 1024, 128)), "x", 0, 0, tiled=True)
     theirs = lax.ppermute(mine, "c", swap)
-
-    def target(step, core):
-        return jnp.where(step < 4, core[0], 1 - core[0]) * 4 + step % 4
-
-    weight_grad, gain_grad = pl.pallas_call(
-        finish_kernel,
-        out_shape=[shape((WIDTH, WIDTH), F32), shape((1, WIDTH), F32)],
-        grid_spec=pltpu.PrefetchScalarGridSpec(
-            num_scalar_prefetch=1,
-            grid=(8,),
-            in_specs=[
-                pl.BlockSpec((1, 64, 16, 128), lambda s, core: (jnp.minimum(s, 3), 0, 0, 0)),
-                pl.BlockSpec((1, 64, 16, 128), lambda s, core: (jnp.maximum(s - 4, 0), 0, 0, 0)),
-                pl.BlockSpec((ROWS, WIDTH), lambda s, core: (target(s, core), 0)),
-                pl.BlockSpec((1, 128), lambda s, core: (0, target(s, core))),
-            ],
-            out_specs=[
-                pl.BlockSpec((ROWS, WIDTH), lambda s, core: (target(s, core), 0)),
-                pl.BlockSpec((1, 128), lambda s, core: (0, target(s, core))),
-            ],
-        ),
-        compiler_params=PARAMS,
-        cost_estimate=pl.CostEstimate(flops=3_000_000, bytes_accessed=8_000_000, transcendentals=0),
-        name="finish",
-    )(core, mine, theirs, out_weight, gain)
+    partial = finish(False, mine, out_weight, gain, ())
+    weight_grad, gain_grad = finish(True, theirs, out_weight, gain, partial)
     return (layer_out, query_grad, key_grad, value_grad, gate_grad, gain_grad.reshape(WIDTH), weight_grad)
 
 

time: 107 us -> 105 us (0.981)
  other arithmetic: 1.54 us -> 0 us
    reduce_sum x2 -> x0, other arithmetic: 1.54 us -> none  [the longest x1 1.47 us: per_device(): block = jnp.sum(pieces.astype(F32), axis=0).astype(BF16)]
    unnamed x18 -> x14, local copies, waits for them, and re-layouts: 3.97 us -> 3 us
    pallas_call x2 -> x5, Pallas kernels: 6.11 us -> 6.23 us  [the longest x2 3.93 us: finish(): pl.pallas_call(finish_kernel, out_shape=[shape((WIDTH, WIDTH), F32), shap...]
  transfers between devices with their start and end apart: 2 -> 2, of which waited for: 1 -> 1; matrix products, arithmetic and copies ran while one was open for 0% -> 0% of each run, Pallas kernels for 4% -> 6%
where the time goes in v2:
time: 105 us; the launch traced here: 104 us
  blocking collectives  71.3 us (68%)
  starting transfers between devices  16.1 us (15%)
  Pallas kernels  10.3 us (10%)
  local copies, waits for them, and re-layouts  3.16 us (3%)
  waiting for transfers between devices  2.64 us (3%)
    all_to_all x1, blocking collectives, per_device(): pieces = lax.all_to_all(block.reshape(64, 16, 128), PLANE, 0, 0, tiled=True)  24 us
    all_to_all x1, blocking collectives, per_device(): pieces = lax.all_to_all(part, 'x', 0, 0, tiled=True)  17.3 us
    all_to_all x1, blocking collectives, per_device(): block = lax.all_to_all(total, PLANE, 0, 0, tiled=True).reshape(1, 1024, 128)  16.5 us
    all_to_all x1, blocking collectives, per_device(): lax.all_to_all(jnp.broadcast_to(block, (4, 1024, 128)), 'x', 0, 0, tiled=...  13.5 us
    ppermute x1, starting transfers between devices, per_device(): other = lax.ppermute(own, 'c', swap)  8.79 us
    ppermute x1, starting transfers between devices, per_device(): theirs = lax.ppermute(mine, 'c', swap)  7.29 us
    pallas_call x1, Pallas kernels, per_device(): pl.pallas_call(backward_kernel, out_shape=[shape((ROWS, WIDTH), BF16)] *...  4.07 us
    pallas_call x2, Pallas kernels, finish(): pl.pallas_call(finish_kernel, out_shape=[shape((WIDTH, WIDTH), F32), shap...  3.93 us
  transfers between devices with their start and end apart: 2, of which 1 were waited for; matrix products, arithmetic and copies ran while one was open for 0% of the time, Pallas kernels for 6%

profile of v2, /device:TPU:1, one launch (start us, length us, event | category | flops | bytes accessed | tf_op | source)
XLA Modules:
  0.0 104.2 jit_solution(15342763415217316575)
XLA Ops:
  0.6 0.0 copy-start.3
  0.6 0.0 copy-start.4
  0.7 0.0 copy-start.2
  0.7 0.0 copy-start.1
  0.7 1.0 constant_dynamic-update-slice_fusion.4
  1.7 1.0 constant_dynamic-update-slice_fusion.3
  2.7 1.0 constant_dynamic-update-slice_fusion.2
  3.6 0.0 copy-done.3
  3.7 8.8 %collective-permute-start = (bf16[640,1024]{1,0:T(8,128)(2,1)S(1)}, bf16[640,1024]{1,0:T(8,128)(2,1)S(1)}, u32[]{:S(2)}, u32[]{:S(2)}) collective-permute-start(bf16[640,1024]{1,0:T(8,128)(2,1)S(1)} %constant_dynamic-update-slice_fusion.own), channel_id=1, source_target_pairs={{0,1},{1,0},{2,3},{3,2},{4,5},{5,4},{6,7},{7,6},{8,9},{9,8},{10,11... | collective-permute-start | bytes 3932168 | tf_op jit(solution)/shard_map/ppermute | solution.py:184
  12.5 2.6 %collective-permute-done.other = bf16[640,1024]{1,0:T(8,128)(2,1)S(1)} collective-permute-done((bf16[640,1024]{1,0:T(8,128)(2,1)S(1)}, bf16[640,1024]{1,0:T(8,128)(2,1)S(1)}, u32[]{:S(2)}, u32[]{:S(2)}) %collective-permute-start) | collective-permute-done | bytes 1310752 | tf_op jit(solution)/shard_map/ppermute | solution.py:184
  15.2 2.1 %forward.1 = (bf16[4,1024,128]{2,1,0:T(8,128)(2,1)S(1)}, f32[256,1024]{1,0:T(8,128)S(1)}, f32[256,1]{1,0:T(8,128)S(1)}, bf16[128,1024]{1,0:T(8,128)(2,1)S(1)}) custom-call(s32[1,4]{1,0:T(1,128)S(1)} %copy-done.2, bf16[640,1024]{1,0:T(8,128)(2,1)S(1)} %constant_dynamic-update-slice_fusion.own, bf16[640,1024]{1,0:T(8,128)(2,1)S(1)} %collective-permute-done.other, ...), custom_call_target="tpu_custom_call" | custom-call | flops 540000000 | bytes 6000000 | tf_op jit(solution)/shard_map/forward/pallas_call | solution.py:185
  17.3 17.3 %all_to_all.20.pieces = bf16[4,1024,128]{2,1,0:T(8,128)(2,1)S(1)} all-to-all(bf16[4,1024,128]{2,1,0:T(8,128)(2,1)S(1)} %get-tuple-element.28), channel_id=1, replica_groups=mesh['z'=8,'y'=8,'x'=4,'c'=2] {'x'}, dimensions={0} | all-to-all | bytes 2097152 | tf_op jit(solution)/shard_map/all_to_all | solution.py:201
  34.6 0.1 chip_sum.1
  34.7 24.0 %all_to_all.21.pieces = bf16[64,16,128]{2,1,0:T(8,128)(2,1)S(1)} all-to-all(bf16[64,16,128]{2,1,0:T(8,128)(2,1)S(1)} %bitcast.4), channel_id=1, replica_groups=mesh['z'=8,'y'=8,'x'=4,'c'=2] {'z','y'}, dimensions={0} | all-to-all | bytes 524288 | tf_op jit(solution)/shard_map/all_to_all | solution.py:222
  58.8 0.1 plane_sum.1
  58.8 16.5 %all_to_all.22 = bf16[64,16,128]{2,1,0:T(8,128)(2,1)S(1)} all-to-all(bf16[64,16,128]{2,1,0:T(8,128)(2,1)S(1)} %plane_sum.1), channel_id=1, replica_groups=mesh['z'=8,'y'=8,'x'=4,'c'=2] {'z','y'}, dimensions={0} | all-to-all | bytes 524288 | tf_op jit(solution)/shard_map/all_to_all | solution.py:231
  75.3 0.1 broadcast_in_dim.8
  75.4 0.0 copy-start
  75.4 13.5 %all_to_all.23.source = bf16[4,1024,128]{2,1,0:T(8,128)(2,1)S(1)} all-to-all(bf16[4,1024,128]{2,1,0:T(8,128)(2,1)S(1)} %broadcast_in_dim.8), channel_id=1, replica_groups=mesh['z'=8,'y'=8,'x'=4,'c'=2] {'x'}, dimensions={0} | all-to-all | bytes 2097152 | tf_op jit(solution)/shard_map/all_to_all | solution.py:232
  88.9 7.3 %collective-permute-start.1 = (bf16[4,1024,128]{2,1,0:T(8,128)(2,1)S(1)}, bf16[4,1024,128]{2,1,0:T(8,128)(2,1)S(1)}, u32[]{:S(2)}, u32[]{:S(2)}) collective-permute-start(bf16[4,1024,128]{2,1,0:T(8,128)(2,1)S(1)} %all_to_all.23.source), channel_id=1, source_target_pairs={{0,1},{1,0},{2,3},{3,2},{4,5},{5,4},{6,7},{7,6},{8,9},{9,8},{10,11... | collective-permute-start | bytes 3145736 | tf_op jit(solution)/shard_map/ppermute | solution.py:233
  96.2 4.1 %backward.1 = (bf16[128,1024]{1,0:T(8,128)(2,1)}, bf16[128,1024]{1,0:T(8,128)(2,1)}, bf16[128,1024]{1,0:T(8,128)(2,1)}, bf16[128,1024]{1,0:T(8,128)(2,1)}, bf16[128,1024]{1,0:T(8,128)(2,1)}) custom-call(s32[1,4]{1,0:T(1,128)S(1)} %copy-done.2, bf16[640,1024]{1,0:T(8,128)(2,1)S(1)} %constant_dynamic-update-slice_fusion.own, ...), custom_call_target="tpu_custom_call" | custom-call | flops 1800000000 | bytes 9000000 | tf_op jit(solution)/shard_map/backward/pallas_call | solution.py:203
  100.3 1.9 %finish_mine.1 = (f32[1024,1024]{1,0:T(8,128)}, f32[1,1024]{1,0:T(1,128)}) custom-call(bf16[4,1024,128]{2,1,0:T(8,128)(2,1)S(1)} %all_to_all.23.source, bf16[1024,1024]{1,0:T(8,128)(2,1)S(1)} %copy-done, f32[1,1024]{1,0:T(1,128)S(1)} %bitcast.7), custom_call_target="tpu_custom_call" | custom-call | flops 1500000 | bytes 4000000 | tf_op jit(solution)/shard_map/finish_mine/pallas_call | solution.py:165
  102.2 0.0 collective-permute-done.1.source
  102.2 2.0 %finish_theirs.1 = (f32[1024,1024]{1,0:T(8,128)}, f32[1,1024]{1,0:T(1,128)}) custom-call(bf16[4,1024,128]{2,1,0:T(8,128)(2,1)S(1)} %collective-permute-done.1.source, bf16[1024,1024]{1,0:T(8,128)(2,1)S(1)} %copy-done, f32[1,1024]{1,0:T(1,128)S(1)} %bitcast.8, f32[1024,1024]{1,0:T(8,128)} %get-tuple-element.29.rest_0_, ...), custom_call_target="tpu_custom_call", output_to_operand_aliasing={{0}: (3, {}), {1}: (4, {})} | custom-call | flops 1500000 | bytes 4000000 | tf_op jit(solution)/shard_map/finish_theirs/pallas_call | solution.py:165
  (6 shorter events, 0.0 us)
Async XLA Ops:
  0.6 3.0 %copy-start.3 = (bf16[128,1024]{1,0:T(8,128)(2,1)S(1)}, bf16[128,1024]{1,0:T(8,128)(2,1)}, u32[]{:S(2)}) copy-start(bf16[128,1024]{1,0:T(8,128)(2,1)} %param.11) | copy-start | bytes 786436
  0.6 3.0 %copy-start.4 = (bf16[128,1024]{1,0:T(8,128)(2,1)S(1)}, bf16[128,1024]{1,0:T(8,128)(2,1)}, u32[]{:S(2)}) copy-start(bf16[128,1024]{1,0:T(8,128)(2,1)} %param.15) | copy-start | bytes 786436
  0.7 14.5 %copy-start.2 = (s32[1,4]{1,0:T(1,128)S(1)}, s32[1,4]{1,0:T(1,128)}, u32[]{:S(2)}) copy-start(s32[1,4]{1,0:T(1,128)} %lengths.3) | copy-start | bytes 52
  0.7 14.5 %copy-start.1 = (f32[1024]{0:T(1024)S(1)}, f32[1024]{0:T(1024)}, u32[]{:S(2)}) copy-start(f32[1024]{0:T(1024)} %param.13) | copy-start | bytes 12292
  3.7 11.4 %collective-permute-start = (bf16[640,1024]{1,0:T(8,128)(2,1)S(1)}, bf16[640,1024]{1,0:T(8,128)(2,1)S(1)}, u32[]{:S(2)}, u32[]{:S(2)}) collective-permute-start(bf16[640,1024]{1,0:T(8,128)(2,1)S(1)} %constant_dynamic-update-slice_fusion.own), channel_id=1, source_target_pairs={{0,1},{1,0},{2,3},{3,2},{4,5},{5,4},{6,7},{7,6},{8,9},{9,8},{10,11... | collective-permute-start | bytes 3932168 | tf_op jit(solution)/shard_map/ppermute | solution.py:184
  75.4 20.8 %copy-start = (bf16[1024,1024]{1,0:T(8,128)(2,1)S(1)}, bf16[1024,1024]{1,0:T(8,128)(2,1)}, u32[]{:S(2)}) copy-start(bf16[1024,1024]{1,0:T(8,128)(2,1)} %weight.5) | copy-start | bytes 6291460
  88.9 13.3 %collective-permute-start.1 = (bf16[4,1024,128]{2,1,0:T(8,128)(2,1)S(1)}, bf16[4,1024,128]{2,1,0:T(8,128)(2,1)S(1)}, u32[]{:S(2)}, u32[]{:S(2)}) collective-permute-start(bf16[4,1024,128]{2,1,0:T(8,128)(2,1)S(1)} %all_to_all.23.source), channel_id=1, source_target_pairs={{0,1},{1,0},{2,3},{3,2},{4,5},{5,4},{6,7},{7,6},{8,9},{9,8},{10,11... | collective-permute-start | bytes 3145736 | tf_op jit(solution)/shard_map/ppermute | solution.py:233

commit v3 on v2

v3 whole, which is shorter than its diff:
```python
import functools

import jax
import jax.numpy as jnp
from jax import lax
from jax.experimental import pallas as pl
from jax.experimental.pallas import tpu as pltpu
from jax.sharding import Mesh, PartitionSpec as P

HEADS = 4
HEAD_DIM = 256
WIDTH = 1024
ROWS = 128
GROUP = 256
PLANE = ("z", "y")
CHIPS = ("z", "y", "x")
DEVICES = ("z", "y", "x", "c")
F32 = jnp.float32
BF16 = jnp.bfloat16
VMEM = pl.BlockSpec(memory_space=pltpu.VMEM)
SMEM = pl.BlockSpec(memory_space=pltpu.SMEM)
PARAMS = pltpu.CompilerParams(vmem_limit_bytes=20 * 1024 * 1024)


def dot(a, b, contract):
    return lax.dot_general(a, b, (contract, ((), ())), preferred_element_type=F32)


def visible(lengths, first_row, first_column, size):
    row = first_row + lax.broadcasted_iota(jnp.int32, (size, 1), 0)
    column = first_column + lax.broadcasted_iota(jnp.int32, (size, size), 1)
    start = jnp.zeros((size, 1), jnp.int32)
    end = 0
    for user in range(3):
        end = end + lengths[0, user]
        start = jnp.where(row >= end, end, start)
    return (column <= row) & (column >= start)


QUERY, KEY, VALUE, GATE, COTANGENT = range(5)


def at(core, item):
    first = core * 5 * ROWS + item * ROWS
    return pl.ds(first if isinstance(core, int) else pl.multiple_of(first, ROWS), ROWS)


def both(whole, item, columns):
    return jnp.concatenate([whole[at(0, item), columns], whole[at(1, item), columns]], axis=0)


def head_columns(head):
    return slice(head * HEAD_DIM, (head + 1) * HEAD_DIM)


def gate_rows_of(first, count):
    core, row = divmod(first, ROWS)
    return pl.ds(core * 5 * ROWS + GATE * ROWS + row, count)


def tile(index):
    return slice(index * 16, (index + 1) * 16)


def forward_kernel(lengths, whole, gain, part, normed, inv_std, gated, attended):
    core = lax.axis_index("c")
    mask = visible(lengths, 0, 0, GROUP)
    for head in range(HEADS):
        columns = head_columns(head)
        scores = dot(both(whole, QUERY, columns), both(whole, KEY, columns), ((1,), (1,))) * (HEAD_DIM**-0.5)
        weights = jnp.where(mask, scores * jax.nn.sigmoid(scores), 0.0).astype(BF16)
        attended[:, columns] = dot(weights, both(whole, VALUE, columns), ((1,), (0,)))
    chunk = 32
    for first in range(0, GROUP, chunk):
        rows = slice(first, first + chunk)
        values = attended[rows, :]
        centered = values - jnp.mean(values, axis=1, keepdims=True)
        inverse = lax.rsqrt(jnp.mean(centered * centered, axis=1, keepdims=True) + 1e-05)
        unit = centered * inverse
        normed[rows, :] = unit
        inv_std[rows, :] = inverse
        result = (unit * gain[...] * whole[gate_rows_of(first, chunk), :].astype(F32)).astype(BF16)
        gated[0, rows, :] = result[:, : WIDTH // 2]
        gated[1, rows, :] = result[:, WIDTH // 2 :]
    for x in range(4):
        mine = gated[core, :, x * 128 : (x + 1) * 128]
        for half in range(2):
            wide = slice(half * 512, (half + 1) * 512)
            block = dot(mine, both(whole, COTANGENT, wide), ((0,), (0,))).astype(BF16)
            for i in range(8):
                for j in range(4):
                    part[x, tile(i * 8 + half * 4 + j), :] = block[i * 16 : (i + 1) * 16, j * 128 : (j + 1) * 128]


def finish_rows(theirs, source, weight, gain, weight_grad, gain_grad, rows_out, gain_out, sems):
    core = lax.axis_index("c")
    half = 1 - core if theirs else core
    copies = []
    for x in range(4):
        first = pl.multiple_of(half * 512 + x * ROWS, ROWS)
        total = jnp.zeros((ROWS, 128), F32)
        for j in range(8):
            columns = slice(j * 128, (j + 1) * 128)
            block = jnp.concatenate([source[x, tile(i * 8 + j), :].astype(F32) for i in range(8)], axis=0)
            rows_out[x * ROWS : (x + 1) * ROWS, columns] = block
            total = total + block * weight[pl.ds(first, ROWS), columns].astype(F32)
        copies.append(
            pltpu.make_async_copy(
                rows_out.at[pl.ds(x * ROWS, ROWS), :], weight_grad.at[pl.ds(first, ROWS), :], sems.at[x]
            )
        )
        copies[-1].start()
        gain_out[:, x * 128 : (x + 1) * 128] = jnp.sum(total.T, axis=0, keepdims=True) / gain[:, pl.ds(first, 128)]
    copies.append(pltpu.make_async_copy(gain_out, gain_grad.at[half], sems.at[4]))
    copies[-1].start()
    return copies


def backward_kernel(
    lengths, whole, gain, normed, inv_std, gated, weight, mine,
    layer_hbm, query_hbm, key_hbm, value_hbm, gate_hbm, weight_grad, gain_grad,
    layer_out, query_grad, key_grad, value_grad, gate_grad, gated_grad, out_grad, rows_out, gain_out, sems,
):
    copies = finish_rows(False, mine, weight, gain, weight_grad, gain_grad, rows_out, gain_out, sems)

    def send(source, target, columns=None):
        if columns is not None:
            source, target = source.at[:, columns], target.at[:, columns]
        copies.append(pltpu.make_async_copy(source, target, sems.at[len(copies)]))
        copies[-1].start()

    core = lax.axis_index("c")
    first_own = pl.multiple_of(core * ROWS, ROWS)
    own_rows = pl.ds(first_own, ROWS)
    scale = HEAD_DIM**-0.5
    gated_grad[...] = dot(both(whole, COTANGENT, slice(None)), weight[...], ((1,), (1,)))
    chunk = 16
    for first in range(0, GROUP, chunk):
        rows = slice(first, first + chunk)
        unit = normed[rows, :]
        scaled = gated_grad[rows, :] * gain[...]
        gate_grad[rows, :] = (scaled * unit).astype(BF16)
        inner = scaled * whole[gate_rows_of(first, chunk), :].astype(F32)
        inner = (
            inner
            - jnp.mean(inner, axis=1, keepdims=True)
            - unit * jnp.mean(inner * unit, axis=1, keepdims=True)
        ) * inv_std[rows, :]
        out_grad[rows, :] = inner.astype(BF16)
    send(gate_grad.at[own_rows, :], gate_hbm)
    layer_out[...] = (
        dot(gated[0, own_rows, :], weight[: WIDTH // 2], ((1,), (0,)))
        + dot(gated[1, own_rows, :], weight[WIDTH // 2 :], ((1,), (0,)))
    ).astype(BF16)
    send(layer_out, layer_hbm)
    mask_own, mask_cross = visible(lengths, first_own, first_own, ROWS), visible(lengths, ROWS, 0, ROWS)
    for head in range(HEADS):
        columns = head_columns(head)

        def block(query_core, key_core, grads, mask):
            query, key = whole[at(query_core, QUERY), columns], whole[at(key_core, KEY), columns]
            scores = dot(query, key, ((1,), (1,))) * scale
            sigma = jax.nn.sigmoid(scores)
            weights = jnp.where(mask, scores * sigma, 0.0).astype(BF16)
            slope = sigma * (1.0 + scores * (1.0 - sigma))
            value_dot = dot(grads, whole[at(key_core, VALUE), columns], ((1,), (1,)))
            score_grad = jnp.where(mask, value_dot * slope, 0.0).astype(BF16)
            return (
                dot(score_grad, key, ((1,), (0,))),
                dot(score_grad, query, ((0,), (0,))),
                dot(weights, grads, ((0,), (0,))),
            )

        query_own, key_own, value_own = block(core, core, out_grad[own_rows, columns], mask_own)
        query_cross, key_cross, value_cross = block(1, 0, out_grad[ROWS:, columns], mask_cross)
        query_sum = query_own + jnp.where(core == 1, query_cross, 0.0)
        key_sum = key_own + jnp.where(core == 0, key_cross, 0.0)
        value_sum = value_own + jnp.where(core == 0, value_cross, 0.0)
        query_grad[:, columns] = (query_sum * scale).astype(BF16)
        key_grad[:, columns] = (key_sum * scale).astype(BF16)
        value_grad[:, columns] = value_sum.astype(BF16)
        send(query_grad, query_hbm, columns)
        send(key_grad, key_hbm, columns)
        send(value_grad, value_hbm, columns)
    for copy in copies:
        copy.wait()


def chip_sum_kernel(pieces, total):
    for first in range(0, 1024, 128):
        rows = slice(first, first + 128)
        value = pieces[0, rows, :].astype(F32) + pieces[1, rows, :].astype(F32)
        total[rows, :] = (value + (pieces[2, rows, :].astype(F32) + pieces[3, rows, :].astype(F32))).astype(BF16)


def plane_sum_kernel(pieces, total):
    sums = [pieces[i].astype(F32) for i in range(4)]
    for first in range(4, 64, 4):
        sums = [sums[i] + pieces[first + i].astype(F32) for i in range(4)]
    value = ((sums[0] + sums[1]) + (sums[2] + sums[3])).astype(BF16)
    for i in range(64):
        total[i] = value


def finish_kernel(source, weight, gain, weight_in, gain_in, weight_grad, gain_grad, rows_out, gain_out, sems):
    for copy in finish_rows(True, source, weight, gain, weight_grad, gain_grad, rows_out, gain_out, sems):
        copy.wait()


def per_device(query_rows, key_rows, value_rows, gate_rows, lengths, norm_gain, out_weight, cotangent):
    gain = norm_gain.reshape(1, WIDTH)
    swap = [(0, 1), (1, 0)]
    shape = jax.ShapeDtypeStruct
    own = jnp.concatenate([query_rows, key_rows, value_rows, gate_rows, cotangent], axis=0)
    whole = lax.all_gather(own, "c", axis=0, tiled=True)
    part, normed, inv_std, gated = pl.pallas_call(
        forward_kernel,
        out_shape=[
            shape((4, 1024, 128), BF16),
            shape((GROUP, WIDTH), F32),
            shape((GROUP, 1), F32),
            shape((2, GROUP, WIDTH // 2), BF16),
        ],
        in_specs=[SMEM, VMEM, VMEM],
        out_specs=[VMEM] * 4,
        scratch_shapes=[pltpu.VMEM((GROUP, WIDTH), F32)],
        compiler_params=PARAMS,
        cost_estimate=pl.CostEstimate(flops=540_000_000, bytes_accessed=6_000_000, transcendentals=300_000),
        name="forward",
    )(lengths, whole, gain)

    pieces = lax.all_to_all(part, "x", 0, 0, tiled=True)

    block = pl.pallas_call(
        chip_sum_kernel,
        out_shape=shape((1024, 128), BF16),
        in_specs=[VMEM],
        out_specs=VMEM,
        compiler_params=PARAMS,
        name="chip_sum",
    )(pieces)
    pieces = lax.all_to_all(block.reshape(64, 16, 128), PLANE, 0, 0, tiled=True)
    total = pl.pallas_call(
        plane_sum_kernel,
        out_shape=shape((64, 16, 128), BF16),
        in_specs=[VMEM],
        out_specs=VMEM,
        compiler_params=PARAMS,
        name="plane_sum",
    )(pieces)
    block = lax.all_to_all(total, PLANE, 0, 0, tiled=True).reshape(1, 1024, 128)
    mine = lax.all_to_all(jnp.broadcast_to(block, (4, 1024, 128)), "x", 0, 0, tiled=True)
    theirs = lax.ppermute(mine, "c", swap)
    anywhere = pl.BlockSpec(memory_space=pl.ANY)
    sums = [shape((WIDTH, WIDTH), F32), shape((2, 1, WIDTH // 2), F32)]
    staging = [pltpu.VMEM((WIDTH // 2, WIDTH), F32), pltpu.VMEM((1, WIDTH // 2), F32)]
    *grads, weight_part, gain_part = pl.pallas_call(
        backward_kernel,
        out_shape=[shape((ROWS, WIDTH), BF16)] * 5 + sums,
        in_specs=[SMEM] + [VMEM] * 7,
        out_specs=[anywhere] * 7,
        scratch_shapes=[pltpu.VMEM((ROWS, WIDTH), BF16)] * 4
        + [pltpu.VMEM((GROUP, WIDTH), BF16)]
        + [pltpu.VMEM((GROUP, WIDTH), F32), pltpu.VMEM((GROUP, WIDTH), BF16)]
        + staging
        + [pltpu.SemaphoreType.DMA((19,))],
        compiler_params=PARAMS,
        cost_estimate=pl.CostEstimate(flops=1_800_000_000, bytes_accessed=9_000_000, transcendentals=300_000),
        name="backward",
    )(lengths, whole, gain, normed, inv_std, gated, out_weight, mine)
    weight_grad, gain_grad = pl.pallas_call(
        finish_kernel,
        out_shape=sums,
        in_specs=[VMEM] * 3 + [anywhere] * 2,
        out_specs=[anywhere] * 2,
        input_output_aliases={3: 0, 4: 1},
        scratch_shapes=staging + [pltpu.SemaphoreType.DMA((5,))],
        compiler_params=PARAMS,
        cost_estimate=pl.CostEstimate(flops=1_500_000, bytes_accessed=4_000_000, transcendentals=0),
        name="finish",
    )(theirs, out_weight, gain, weight_part, gain_part)
    return (*grads, gain_grad.reshape(WIDTH), weight_grad)


def solution(mesh):
    chips = Mesh(mesh.devices.reshape(8, 8, 4, 2), DEVICES)
    rows = P(DEVICES, None)
    return jax.shard_map(
        per_device,
        mesh=chips,
        in_specs=(rows, rows, rows, rows, P(CHIPS, None), P(), P(), rows),
        out_specs=(rows, rows, rows, rows, rows, P(), P()),
        check_vma=False,
    )
```

time: 105 us -> 138 us (1.31)
  waiting for transfers between devices: 2.64 us -> 26.6 us
  between operations: 0.76 us -> 14.2 us
  starting transfers between devices: 16.1 us -> 6.6 us
  blocking collectives: 71.3 us -> 74.8 us
  local copies, waits for them, and re-layouts: 3.16 us -> 5.95 us
    all_gather x0 -> x1, waiting for transfers between devices: none -> 26.6 us  [per_device(): whole = lax.all_gather(own, 'c', axis=0, tiled=True)]
    ppermute x1 -> x0, starting transfers between devices: 8.79 us -> none  [per_device(): other = lax.ppermute(own, 'c', swap)]
    unnamed x14 -> x20, local copies, waits for them, and re-layouts: 3 us -> 5.8 us
    ppermute x1 -> x0, waiting for transfers between devices: 2.64 us -> none  [per_device(): other = lax.ppermute(own, 'c', swap)]
    pallas_call x2 -> x1, Pallas kernels: 3.93 us -> 1.63 us  [per_device(): pl.pallas_call(finish_kernel, out_shape=sums, in_specs=[VMEM] * 3 + [anyw...]
    all_to_all x1, blocking collectives: 16.5 us -> 17.9 us  [per_device(): block = lax.all_to_all(total, PLANE, 0, 0, tiled=True).reshape(1, 1024, 128)]
    all_to_all x1, blocking collectives: 24 us -> 25.4 us  [per_device(): pieces = lax.all_to_all(block.reshape(64, 16, 128), PLANE, 0, 0, tiled=True)]
  transfers between devices with their start and end apart: 2 -> 2, of which waited for: 1 -> 1; matrix products, arithmetic and copies ran while one was open for 0% -> 0% of each run, Pallas kernels for 6% -> 4%
where the time goes in v3:
time: 138 us; the launch traced here: 137 us
  blocking collectives  74.8 us (54%)
  waiting for transfers between devices  26.6 us (19%)
  between operations  14.2 us (10%)
  Pallas kernels  9.01 us (7%)
  starting transfers between devices  6.6 us (5%)
  local copies, waits for them, and re-layouts  5.95 us (4%)
    all_gather x1, waiting for transfers between devices, per_device(): whole = lax.all_gather(own, 'c', axis=0, tiled=True)  26.6 us
    all_to_all x1, blocking collectives, per_device(): pieces = lax.all_to_all(block.reshape(64, 16, 128), PLANE, 0, 0, tiled=True)  25.4 us
    all_to_all x1, blocking collectives, per_device(): block = lax.all_to_all(total, PLANE, 0, 0, tiled=True).reshape(1, 1024, 128)  17.9 us
    all_to_all x1, blocking collectives, per_device(): pieces = lax.all_to_all(part, 'x', 0, 0, tiled=True)  17.5 us
    all_to_all x1, blocking collectives, per_device(): lax.all_to_all(jnp.broadcast_to(block, (4, 1024, 128)), 'x', 0, 0, tiled=...  13.9 us
    ppermute x1, starting transfers between devices, per_device(): theirs = lax.ppermute(mine, 'c', swap)  6.56 us
    unnamed x20, local copies, waits for them, and re-layouts  5.8 us
    pallas_call x1, Pallas kernels, per_device(): pl.pallas_call(backward_kernel, out_shape=[shape((ROWS, WIDTH), BF16)] *...  5.11 us
  transfers between devices with their start and end apart: 2, of which 1 were waited for; matrix products, arithmetic and copies ran while one was open for 0% of the time, Pallas kernels for 4%

profile of v3, /device:TPU:1, one launch (start us, length us, event | category | flops | bytes accessed | tf_op | source)
XLA Modules:
  0.0 137.2 jit_solution(6547789714333271047)
XLA Ops:
  7.2 0.0 all-gather.2.cloned.1.call-start
  7.2 1.0 constant_dynamic-update-slice_fusion.4
  8.3 1.0 constant_dynamic-update-slice_fusion.3
  9.2 1.0 constant_dynamic-update-slice_fusion.2
  10.2 0.0 copy-start.3
  10.2 0.0 copy-start.4
  10.3 0.0 copy-start.5
  10.3 1.0 copy-done.5
  11.4 0.0 all-gather.2.cloned.1.call-update
  11.4 26.6 %all-gather.2.cloned.1.call-done.whole = bf16[1280,1024]{1,0:T(8,128)(2,1)} async-done(((bf16[640,1024]{1,0:T(8,128)(2,1)}), bf16[1280,1024]{1,0:T(8,128)(2,1)}) %all-gather.2.cloned.1.call-update) | async-done | bytes 2621456 | tf_op jit(solution)/shard_map/all_gather | solution.py:215
  38.0 1.7 %copy-done = bf16[1280,1024]{1,0:T(8,128)(2,1)S(1)} copy-done((bf16[1280,1024]{1,0:T(8,128)(2,1)S(1)}, bf16[1280,1024]{1,0:T(8,128)(2,1)}, u32[]{:S(2)}) %copy-start) | copy-done | bytes 2621464
  39.7 2.1 %forward.1 = (bf16[4,1024,128]{2,1,0:T(8,128)(2,1)S(1)}, f32[256,1024]{1,0:T(8,128)S(1)}, f32[256,1]{1,0:T(8,128)S(1)}, bf16[2,256,512]{2,1,0:T(8,128)(2,1)S(1)}) custom-call(s32[1,4]{1,0:T(1,128)S(1)} %copy-done.4, bf16[1280,1024]{1,0:T(8,128)(2,1)S(1)} %copy-done, f32[1,1024]{1,0:T(1,128)S(1)} %bitcast.5), custom_call_target="tpu_custom_call" | custom-call | flops 540000000 | bytes 6000000 | tf_op jit(solution)/shard_map/forward/pallas_call | solution.py:216
  41.8 17.5 %all_to_all.20.pieces = bf16[4,1024,128]{2,1,0:T(8,128)(2,1)S(1)} all-to-all(bf16[4,1024,128]{2,1,0:T(8,128)(2,1)S(1)} %get-tuple-element.23), channel_id=1, replica_groups=mesh['z'=8,'y'=8,'x'=4,'c'=2] {'x'}, dimensions={0} | all-to-all | bytes 2097152 | tf_op jit(solution)/shard_map/all_to_all | solution.py:232
  59.3 0.1 chip_sum.1
  59.4 0.0 copy-start.2
  59.5 25.4 %all_to_all.21.pieces = bf16[64,16,128]{2,1,0:T(8,128)(2,1)S(1)} all-to-all(bf16[64,16,128]{2,1,0:T(8,128)(2,1)S(1)} %bitcast.4), channel_id=1, replica_groups=mesh['z'=8,'y'=8,'x'=4,'c'=2] {'z','y'}, dimensions={0} | all-to-all | bytes 524288 | tf_op jit(solution)/shard_map/all_to_all | solution.py:242
  84.9 0.1 plane_sum.1
  85.0 17.9 %all_to_all.22 = bf16[64,16,128]{2,1,0:T(8,128)(2,1)S(1)} all-to-all(bf16[64,16,128]{2,1,0:T(8,128)(2,1)S(1)} %plane_sum.1), channel_id=1, replica_groups=mesh['z'=8,'y'=8,'x'=4,'c'=2] {'z','y'}, dimensions={0} | all-to-all | bytes 524288 | tf_op jit(solution)/shard_map/all_to_all | solution.py:251
  102.9 0.1 broadcast_in_dim.8
  103.0 13.9 %all_to_all.23.mine = bf16[4,1024,128]{2,1,0:T(8,128)(2,1)S(1)} all-to-all(bf16[4,1024,128]{2,1,0:T(8,128)(2,1)S(1)} %broadcast_in_dim.8), channel_id=1, replica_groups=mesh['z'=8,'y'=8,'x'=4,'c'=2] {'x'}, dimensions={0} | all-to-all | bytes 2097152 | tf_op jit(solution)/shard_map/all_to_all | solution.py:252
  117.0 6.6 %collective-permute-start = (bf16[4,1024,128]{2,1,0:T(8,128)(2,1)S(1)}, bf16[4,1024,128]{2,1,0:T(8,128)(2,1)S(1)}, u32[]{:S(2)}, u32[]{:S(2)}) collective-permute-start(bf16[4,1024,128]{2,1,0:T(8,128)(2,1)S(1)} %all_to_all.23.mine), channel_id=1, source_target_pairs={{0,1},{1,0},{2,3},{3,2},{4,5},{5,4},{6,7},{7,6},{8,9},{9,8},{10,11... | collective-permute-start | bytes 3145736 | tf_op jit(solution)/shard_map/ppermute | solution.py:253
  123.6 5.1 %backward.1 = (bf16[128,1024]{1,0:T(8,128)(2,1)}, bf16[128,1024]{1,0:T(8,128)(2,1)}, bf16[128,1024]{1,0:T(8,128)(2,1)}, bf16[128,1024]{1,0:T(8,128)(2,1)}, bf16[...) custom-call(s32[1,4]{1,0:T(1,128)S(1)} %copy-done.4, bf16[1280,1024]{1,0:T(8,128)(2,1)S(1)} %copy-done.1, ...), custom_call_target="tpu_custom_call" | custom-call | flops 1800000000 | bytes 9000000 | tf_op jit(solution)/shard_map/backward/pallas_call | solution.py:257
  128.7 0.0 collective-permute-done.source
  128.7 1.6 %finish.1 = (f32[1024,1024]{1,0:T(8,128)}, f32[2,1,512]{2,1,0:T(1,128)}) custom-call(bf16[4,1024,128]{2,1,0:T(8,128)(2,1)S(1)} %collective-permute-done.source, bf16[1024,1024]{1,0:T(8,128)(2,1)S(1)} %copy-done.2, f32[1,1024]{1,0:T(1,128)S(1)} %bitcast.7, f32[1024,1024]{1,0:T(8,128)} %get-tuple-element.29.weight_in, ...), custom_call_target="tpu_custom_call", output_to_operand_aliasing={{0}: (3, {}), {1}: (4, {})} | custom-call | flops 1500000 | bytes 4000000 | tf_op jit(solution)/shard_map/finish/pallas_call | solution.py:271
  (12 shorter events, 0.1 us)
Async XLA Ops:
  7.2 3.0 %copy-start.6 = (bf16[128,1024]{1,0:T(8,128)(2,1)S(1)}, bf16[128,1024]{1,0:T(8,128)(2,1)}, u32[]{:S(2)}) copy-start(bf16[128,1024]{1,0:T(8,128)(2,1)} %param.11) | copy-start | bytes 786436
  7.2 3.1 %copy-start.7 = (bf16[128,1024]{1,0:T(8,128)(2,1)S(1)}, bf16[128,1024]{1,0:T(8,128)(2,1)}, u32[]{:S(2)}) copy-start(bf16[128,1024]{1,0:T(8,128)(2,1)} %param.15) | copy-start | bytes 786436
  7.2 30.8 %all-gather.2.cloned.1.call-start = ((), (), s32[]{:S(2)}) async-start(), calls=%async_computation.4 | async-start | bytes 3932160 | tf_op jit(solution)/shard_map/all_gather | solution.py:215
  10.2 27.8 %copy-start.3 = (f32[1024]{0:T(1024)S(1)}, f32[1024]{0:T(1024)}, u32[]{:S(2)}) copy-start(f32[1024]{0:T(1024)} %param.13) | copy-start | bytes 12292
  10.2 27.8 %copy-start.4 = (s32[1,4]{1,0:T(1,128)S(1)}, s32[1,4]{1,0:T(1,128)}, u32[]{:S(2)}) copy-start(s32[1,4]{1,0:T(1,128)} %lengths.3) | copy-start | bytes 52
  10.3 1.1 copy-start.5
  38.0 1.7 %copy-start = (bf16[1280,1024]{1,0:T(8,128)(2,1)S(1)}, bf16[1280,1024]{1,0:T(8,128)(2,1)}, u32[]{:S(2)}) copy-start(bf16[1280,1024]{1,0:T(8,128)(2,1)} %all-gather.2.cloned.1.call-done.whole) | copy-start | bytes 7864324
  59.4 64.1 %copy-start.2 = (bf16[1024,1024]{1,0:T(8,128)(2,1)S(1)}, bf16[1024,1024]{1,0:T(8,128)(2,1)}, u32[]{:S(2)}) copy-start(bf16[1024,1024]{1,0:T(8,128)(2,1)} %weight.3) | copy-start | bytes 6291460
  102.9 20.7 %copy-start.1 = (bf16[1280,1024]{1,0:T(8,128)(2,1)S(1)}, bf16[1280,1024]{1,0:T(8,128)(2,1)}, u32[]{:S(2)}) copy-start(bf16[1280,1024]{1,0:T(8,128)(2,1)} %all-gather.2.cloned.1.call-done.whole) | copy-start | bytes 7864324
  117.0 11.7 %collective-permute-start = (bf16[4,1024,128]{2,1,0:T(8,128)(2,1)S(1)}, bf16[4,1024,128]{2,1,0:T(8,128)(2,1)S(1)}, u32[]{:S(2)}, u32[]{:S(2)}) collective-permute-start(bf16[4,1024,128]{2,1,0:T(8,128)(2,1)S(1)} %all_to_all.23.mine), channel_id=1, source_target_pairs={{0,1},{1,0},{2,3},{3,2},{4,5},{5,4},{6,7},{7,6},{8,9},{9,8},{10,11... | collective-permute-start | bytes 3145736 | tf_op jit(solution)/shard_map/ppermute | solution.py:253
Sparse Core Ops, SparseCore 0:
  11.5 26.4 all-gather.1

commit v4 on v3

--- a/solution.py
+++ b/solution.py
@@ -26,10 +26,13 @@
     return lax.dot_general(a, b, (contract, ((), ())), preferred_element_type=F32)
 
 
-def visible(lengths, first_row, first_column, size):
-    row = first_row + lax.broadcasted_iota(jnp.int32, (size, 1), 0)
-    column = first_column + lax.broadcasted_iota(jnp.int32, (size, size), 1)
-    start = jnp.zeros((size, 1), jnp.int32)
+def visible_mask(core, lengths):
+    def place(shape, axis):
+        local = lax.broadcasted_iota(jnp.int32, shape, axis)
+        return jnp.where(local < ROWS, core * ROWS + local, (1 - core) * ROWS + local - ROWS)
+
+    row, column = place((GROUP, 1), 0), place((GROUP, GROUP), 1)
+    start = jnp.zeros((GROUP, 1), jnp.int32)
     end = 0
     for user in range(3):
         end = end + lengths[0, user]
@@ -37,39 +40,27 @@
     return (column <= row) & (column >= start)
 
 
-QUERY, KEY, VALUE, GATE, COTANGENT = range(5)
-
-
-def at(core, item):
-    first = core * 5 * ROWS + item * ROWS
-    return pl.ds(first if isinstance(core, int) else pl.multiple_of(first, ROWS), ROWS)
-
-
-def both(whole, item, columns):
-    return jnp.concatenate([whole[at(0, item), columns], whole[at(1, item), columns]], axis=0)
+def both(own, other, item, columns):
+    rows = slice(item * ROWS, (item + 1) * ROWS)
+    return jnp.concatenate([own[rows, columns], other[rows, columns]], axis=0)
 
 
 def head_columns(head):
     return slice(head * HEAD_DIM, (head + 1) * HEAD_DIM)
 
 
-def gate_rows_of(first, count):
-    core, row = divmod(first, ROWS)
-    return pl.ds(core * 5 * ROWS + GATE * ROWS + row, count)
-
-
 def tile(index):
     return slice(index * 16, (index + 1) * 16)
 
 
-def forward_kernel(lengths, whole, gain, part, normed, inv_std, gated, attended):
+def forward_kernel(lengths, own, other, gain, part, normed, inv_std, gated_own, attended, gated):
     core = lax.axis_index("c")
-    mask = visible(lengths, 0, 0, GROUP)
+    visible = visible_mask(core, lengths)
     for head in range(HEADS):
         columns = head_columns(head)
-        scores = dot(both(whole, QUERY, columns), both(whole, KEY, columns), ((1,), (1,))) * (HEAD_DIM**-0.5)
-        weights = jnp.where(mask, scores * jax.nn.sigmoid(scores), 0.0).astype(BF16)
-        attended[:, columns] = dot(weights, both(whole, VALUE, columns), ((1,), (0,)))
+        scores = dot(both(own, other, 0, columns), both(own, other, 1, columns), ((1,), (1,))) * (HEAD_DIM**-0.5)
+        weights = jnp.where(visible, scores * jax.nn.sigmoid(scores), 0.0).astype(BF16)
+        attended[:, columns] = dot(weights, both(own, other, 2, columns), ((1,), (0,)))
     chunk = 32
     for first in range(0, GROUP, chunk):
         rows = slice(first, first + chunk)
@@ -79,14 +70,18 @@
         unit = centered * inverse
         normed[rows, :] = unit
         inv_std[rows, :] = inverse
-        result = (unit * gain[...] * whole[gate_rows_of(first, chunk), :].astype(F32)).astype(BF16)
+        source, at = (own, first) if first < ROWS else (other, first - ROWS)
+        gate = source[3 * ROWS + at : 3 * ROWS + at + chunk, :].astype(F32)
+        result = (unit * gain[...] * gate).astype(BF16)
         gated[0, rows, :] = result[:, : WIDTH // 2]
         gated[1, rows, :] = result[:, WIDTH // 2 :]
+        if first < ROWS:
+            gated_own[rows, :] = result
     for x in range(4):
         mine = gated[core, :, x * 128 : (x + 1) * 128]
         for half in range(2):
             wide = slice(half * 512, (half + 1) * 512)
-            block = dot(mine, both(whole, COTANGENT, wide), ((0,), (0,))).astype(BF16)
+            block = dot(mine, both(own, other, 4, wide), ((0,), (0,))).astype(BF16)
             for i in range(8):
                 for j in range(4):
                     part[x, tile(i * 8 + half * 4 + j), :] = block[i * 16 : (i + 1) * 16, j * 128 : (j + 1) * 128]
@@ -117,7 +112,7 @@
 
 
 def backward_kernel(
-    lengths, whole, gain, normed, inv_std, gated, weight, mine,
+    lengths, own, other, gain, normed, inv_std, gated_own, weight, mine,
     layer_hbm, query_hbm, key_hbm, value_hbm, gate_hbm, weight_grad, gain_grad,
     layer_out, query_grad, key_grad, value_grad, gate_grad, gated_grad, out_grad, rows_out, gain_out, sems,
 ):
@@ -129,56 +124,40 @@
         copies.append(pltpu.make_async_copy(source, target, sems.at[len(copies)]))
         copies[-1].start()
 
-    core = lax.axis_index("c")
-    first_own = pl.multiple_of(core * ROWS, ROWS)
-    own_rows = pl.ds(first_own, ROWS)
     scale = HEAD_DIM**-0.5
-    gated_grad[...] = dot(both(whole, COTANGENT, slice(None)), weight[...], ((1,), (1,)))
+    gated_grad[...] = dot(both(own, other, 4, slice(None)), weight[...], ((1,), (1,)))
     chunk = 16
     for first in range(0, GROUP, chunk):
         rows = slice(first, first + chunk)
         unit = normed[rows, :]
+        source, at = (own, first) if first < ROWS else (other, first - ROWS)
+        gate = source[3 * ROWS + at : 3 * ROWS + at + chunk, :].astype(F32)
         scaled = gated_grad[rows, :] * gain[...]
-        gate_grad[rows, :] = (scaled * unit).astype(BF16)
-        inner = scaled * whole[gate_rows_of(first, chunk), :].astype(F32)
+        if first < ROWS:
+            gate_grad[rows, :] = (scaled * unit).astype(BF16)
+        inner = scaled * gate
         inner = (
             inner
             - jnp.mean(inner, axis=1, keepdims=True)
             - unit * jnp.mean(inner * unit, axis=1, keepdims=True)
         ) * inv_std[rows, :]
         out_grad[rows, :] = inner.astype(BF16)
-    send(gate_grad.at[own_rows, :], gate_hbm)
-    layer_out[...] = (
-        dot(gated[0, own_rows, :], weight[: WIDTH // 2], ((1,), (0,)))
-        + dot(gated[1, own_rows, :], weight[WIDTH // 2 :], ((1,), (0,)))
-    ).astype(BF16)
+    send(gate_grad, gate_hbm)
+    layer_out[...] = dot(gated_own[...], weight[...], ((1,), (0,))).astype(BF16)
     send(layer_out, layer_hbm)
-    mask_own, mask_cross = visible(lengths, first_own, first_own, ROWS), visible(lengths, ROWS, 0, ROWS)
+    visible = visible_mask(lax.axis_index("c"), lengths)
     for head in range(HEADS):
         columns = head_columns(head)
-
-        def block(query_core, key_core, grads, mask):
-            query, key = whole[at(query_core, QUERY), columns], whole[at(key_core, KEY), columns]
-            scores = dot(query, key, ((1,), (1,))) * scale
-            sigma = jax.nn.sigmoid(scores)
-            weights = jnp.where(mask, scores * sigma, 0.0).astype(BF16)
-            slope = sigma * (1.0 + scores * (1.0 - sigma))
-            value_dot = dot(grads, whole[at(key_core, VALUE), columns], ((1,), (1,)))
-            score_grad = jnp.where(mask, value_dot * slope, 0.0).astype(BF16)
-            return (
-                dot(score_grad, key, ((1,), (0,))),
-                dot(score_grad, query, ((0,), (0,))),
-                dot(weights, grads, ((0,), (0,))),
-            )
-
-        query_own, key_own, value_own = block(core, core, out_grad[own_rows, columns], mask_own)
-        query_cross, key_cross, value_cross = block(1, 0, out_grad[ROWS:, columns], mask_cross)
-        query_sum = query_own + jnp.where(core == 1, query_cross, 0.0)
-        key_sum = key_own + jnp.where(core == 0, key_cross, 0.0)
-        value_sum = value_own + jnp.where(core == 0, value_cross, 0.0)
-        query_grad[:, columns] = (query_sum * scale).astype(BF16)
-        key_grad[:, columns] = (key_sum * scale).astype(BF16)
-        value_grad[:, columns] = value_sum.astype(BF16)
+        queries, keys = both(own, other, 0, columns), both(own, other, 1, columns)
+        values, grads = both(own, other, 2, columns), out_grad[:, columns]
+        scores = dot(queries, keys, ((1,), (1,))) * scale
+        sigma = jax.nn.sigmoid(scores)
+        weights = jnp.where(visible, scores * sigma, 0.0).astype(BF16)
+        slope = sigma * (1.0 + scores * (1.0 - sigma))
+        score_grad = jnp.where(visible, dot(grads, values, ((1,), (1,))) * slope, 0.0).astype(BF16)
+        query_grad[:, columns] = (dot(score_grad[:ROWS, :], keys, ((1,), (0,))) * scale).astype(BF16)
+        key_grad[:, columns] = (dot(score_grad[:, :ROWS], queries, ((0,), (0,))) * scale).astype(BF16)
+        value_grad[:, columns] = dot(weights[:, :ROWS], grads, ((0,), (0,))).astype(BF16)
         send(query_grad, query_hbm, columns)
         send(key_grad, key_hbm, columns)
         send(value_grad, value_hbm, columns)
@@ -212,22 +191,22 @@
     swap = [(0, 1), (1, 0)]
     shape = jax.ShapeDtypeStruct
     own = jnp.concatenate([query_rows, key_rows, value_rows, gate_rows, cotangent], axis=0)
-    whole = lax.all_gather(own, "c", axis=0, tiled=True)
-    part, normed, inv_std, gated = pl.pallas_call(
+    other = lax.ppermute(own, "c", swap)
+    part, normed, inv_std, gated_own = pl.pallas_call(
         forward_kernel,
         out_shape=[
             shape((4, 1024, 128), BF16),
             shape((GROUP, WIDTH), F32),
             shape((GROUP, 1), F32),
-            shape((2, GROUP, WIDTH // 2), BF16),
+            shape((ROWS, WIDTH), BF16),
         ],
-        in_specs=[SMEM, VMEM, VMEM],
+        in_specs=[SMEM, VMEM, VMEM, VMEM],
         out_specs=[VMEM] * 4,
-        scratch_shapes=[pltpu.VMEM((GROUP, WIDTH), F32)],
+        scratch_shapes=[pltpu.VMEM((GROUP, WIDTH), F32), pltpu.VMEM((2, GROUP, WIDTH // 2), BF16)],
         compiler_params=PARAMS,
         cost_estimate=pl.CostEstimate(flops=540_000_000, bytes_accessed=6_000_000, transcendentals=300_000),
         name="forward",
-    )(lengths, whole, gain)
+    )(lengths, own, other, gain)
 
     pieces = lax.all_to_all(part, "x", 0, 0, tiled=True)
 
@@ -257,17 +236,16 @@
     *grads, weight_part, gain_part = pl.pallas_call(
         backward_kernel,
         out_shape=[shape((ROWS, WIDTH), BF16)] * 5 + sums,
-        in_specs=[SMEM] + [VMEM] * 7,
+        in_specs=[SMEM] + [VMEM] * 8,
         out_specs=[anywhere] * 7,
-        scratch_shapes=[pltpu.VMEM((ROWS, WIDTH), BF16)] * 4
-        + [pltpu.VMEM((GROUP, WIDTH), BF16)]
+        scratch_shapes=[pltpu.VMEM((ROWS, WIDTH), BF16)] * 5
         + [pltpu.VMEM((GROUP, WIDTH), F32), pltpu.VMEM((GROUP, WIDTH), BF16)]
         + staging
         + [pltpu.SemaphoreType.DMA((19,))],
         compiler_params=PARAMS,
         cost_estimate=pl.CostEstimate(flops=1_800_000_000, bytes_accessed=9_000_000, transcendentals=300_000),
         name="backward",
-    )(lengths, whole, gain, normed, inv_std, gated, out_weight, mine)
+    )(lengths, own, other, gain, normed, inv_std, gated_own, out_weight, mine)
     weight_grad, gain_grad = pl.pallas_call(
         finish_kernel,
         out_shape=sums,

time: 138 us -> 103 us (0.75)
  waiting for transfers between devices: 26.6 us -> 2.64 us
  between operations: 14.2 us -> 0.77 us
  starting transfers between devices: 6.6 us -> 16.1 us
  blocking collectives: 74.8 us -> 71.3 us
  local copies, waits for them, and re-layouts: 5.95 us -> 3.16 us
    all_gather x1 -> x0, waiting for transfers between devices: 26.6 us -> none  [per_device(): whole = lax.all_gather(own, 'c', axis=0, tiled=True)]
    ppermute x0 -> x1, starting transfers between devices: none -> 8.79 us  [per_device(): other = lax.ppermute(own, 'c', swap)]
    unnamed x20 -> x14, local copies, waits for them, and re-layouts: 5.8 us -> 3 us
    ppermute x0 -> x1, waiting for transfers between devices: none -> 2.64 us  [per_device(): other = lax.ppermute(own, 'c', swap)]
    all_to_all x1, blocking collectives: 17.9 us -> 16.5 us  [per_device(): block = lax.all_to_all(total, PLANE, 0, 0, tiled=True).reshape(1, 1024, 128)]
    all_to_all x1, blocking collectives: 25.4 us -> 24 us  [per_device(): pieces = lax.all_to_all(block.reshape(64, 16, 128), PLANE, 0, 0, tiled=True)]
  transfers between devices with their start and end apart: 2 -> 2, of which waited for: 1 -> 1; matrix products, arithmetic and copies ran while one was open for 0% -> 0% of each run, Pallas kernels for 4% -> 5%
where the time goes in v4:
time: 103 us
  blocking collectives  71.3 us (69%)
  starting transfers between devices  16.1 us (16%)
  Pallas kernels  9.17 us (9%)
  local copies, waits for them, and re-layouts  3.16 us (3%)
  waiting for transfers between devices  2.64 us (3%)
    all_to_all x1, blocking collectives, per_device(): pieces = lax.all_to_all(block.reshape(64, 16, 128), PLANE, 0, 0, tiled=True)  24 us
    all_to_all x1, blocking collectives, per_device(): pieces = lax.all_to_all(part, 'x', 0, 0, tiled=True)  17.3 us
    all_to_all x1, blocking collectives, per_device(): block = lax.all_to_all(total, PLANE, 0, 0, tiled=True).reshape(1, 1024, 128)  16.5 us
    all_to_all x1, blocking collectives, per_device(): lax.all_to_all(jnp.broadcast_to(block, (4, 1024, 128)), 'x', 0, 0, tiled=...  13.5 us
    ppermute x1, starting transfers between devices, per_device(): other = lax.ppermute(own, 'c', swap)  8.79 us
    ppermute x1, starting transfers between devices, per_device(): theirs = lax.ppermute(mine, 'c', swap)  7.29 us
    pallas_call x1, Pallas kernels, per_device(): pl.pallas_call(backward_kernel, out_shape=[shape((ROWS, WIDTH), BF16)] *...  5.22 us
    unnamed x14, local copies, waits for them, and re-layouts  3 us
  transfers between devices with their start and end apart: 2, of which 1 were waited for; matrix products, arithmetic and copies ran while one was open for 0% of the time, Pallas kernels for 5%

profile of v4, /device:TPU:1, one launch (start us, length us, event | category | flops | bytes accessed | tf_op | source)
XLA Modules:
  0.0 103.1 jit_solution(16917129204462188316)
XLA Ops:
  0.6 0.0 copy-start.3
  0.6 0.0 copy-start.4
  0.7 0.0 copy-start.2
  0.7 0.0 copy-start.1
  0.7 1.0 constant_dynamic-update-slice_fusion.4
  1.7 1.0 constant_dynamic-update-slice_fusion.3
  2.7 1.0 constant_dynamic-update-slice_fusion.2
  3.7 8.8 %collective-permute-start = (bf16[640,1024]{1,0:T(8,128)(2,1)S(1)}, bf16[640,1024]{1,0:T(8,128)(2,1)S(1)}, u32[]{:S(2)}, u32[]{:S(2)}) collective-permute-start(bf16[640,1024]{1,0:T(8,128)(2,1)S(1)} %constant_dynamic-update-slice_fusion.own), channel_id=1, source_target_pairs={{0,1},{1,0},{2,3},{3,2},{4,5},{5,4},{6,7},{7,6},{8,9},{9,8},{10,11... | collective-permute-start | bytes 3932168 | tf_op jit(solution)/shard_map/ppermute | solution.py:194
  12.5 2.6 %collective-permute-done.other = bf16[640,1024]{1,0:T(8,128)(2,1)S(1)} collective-permute-done((bf16[640,1024]{1,0:T(8,128)(2,1)S(1)}, bf16[640,1024]{1,0:T(8,128)(2,1)S(1)}, u32[]{:S(2)}, u32[]{:S(2)}) %collective-permute-start) | collective-permute-done | bytes 1310752 | tf_op jit(solution)/shard_map/ppermute | solution.py:194
  15.2 0.0 copy-done.2
  15.2 2.1 %forward.1 = (bf16[4,1024,128]{2,1,0:T(8,128)(2,1)S(1)}, f32[256,1024]{1,0:T(8,128)S(1)}, f32[256,1]{1,0:T(8,128)S(1)}, bf16[128,1024]{1,0:T(8,128)(2,1)S(1)}) custom-call(s32[1,4]{1,0:T(1,128)S(1)} %copy-done.2, bf16[640,1024]{1,0:T(8,128)(2,1)S(1)} %constant_dynamic-update-slice_fusion.own, bf16[640,1024]{1,0:T(8,128)(2,1)S(1)} %collective-permute-done.other, ...), custom_call_target="tpu_custom_call" | custom-call | flops 540000000 | bytes 6000000 | tf_op jit(solution)/shard_map/forward/pallas_call | solution.py:195
  17.3 17.3 %all_to_all.20.pieces = bf16[4,1024,128]{2,1,0:T(8,128)(2,1)S(1)} all-to-all(bf16[4,1024,128]{2,1,0:T(8,128)(2,1)S(1)} %get-tuple-element.23), channel_id=1, replica_groups=mesh['z'=8,'y'=8,'x'=4,'c'=2] {'x'}, dimensions={0} | all-to-all | bytes 2097152 | tf_op jit(solution)/shard_map/all_to_all | solution.py:211
  34.6 0.1 chip_sum.1
  34.7 24.0 %all_to_all.21.pieces = bf16[64,16,128]{2,1,0:T(8,128)(2,1)S(1)} all-to-all(bf16[64,16,128]{2,1,0:T(8,128)(2,1)S(1)} %bitcast.4), channel_id=1, replica_groups=mesh['z'=8,'y'=8,'x'=4,'c'=2] {'z','y'}, dimensions={0} | all-to-all | bytes 524288 | tf_op jit(solution)/shard_map/all_to_all | solution.py:221
  58.8 0.1 plane_sum.1
  58.8 16.5 %all_to_all.22 = bf16[64,16,128]{2,1,0:T(8,128)(2,1)S(1)} all-to-all(bf16[64,16,128]{2,1,0:T(8,128)(2,1)S(1)} %plane_sum.1), channel_id=1, replica_groups=mesh['z'=8,'y'=8,'x'=4,'c'=2] {'z','y'}, dimensions={0} | all-to-all | bytes 524288 | tf_op jit(solution)/shard_map/all_to_all | solution.py:230
  75.3 0.1 broadcast_in_dim.8
  75.4 0.0 copy-start
  75.4 13.5 %all_to_all.23.mine = bf16[4,1024,128]{2,1,0:T(8,128)(2,1)S(1)} all-to-all(bf16[4,1024,128]{2,1,0:T(8,128)(2,1)S(1)} %broadcast_in_dim.8), channel_id=1, replica_groups=mesh['z'=8,'y'=8,'x'=4,'c'=2] {'x'}, dimensions={0} | all-to-all | bytes 2097152 | tf_op jit(solution)/shard_map/all_to_all | solution.py:231
  88.9 7.3 %collective-permute-start.1 = (bf16[4,1024,128]{2,1,0:T(8,128)(2,1)S(1)}, bf16[4,1024,128]{2,1,0:T(8,128)(2,1)S(1)}, u32[]{:S(2)}, u32[]{:S(2)}) collective-permute-start(bf16[4,1024,128]{2,1,0:T(8,128)(2,1)S(1)} %all_to_all.23.mine), channel_id=1, source_target_pairs={{0,1},{1,0},{2,3},{3,2},{4,5},{5,4},{6,7},{7,6},{8,9},{9,8},{10,11... | collective-permute-start | bytes 3145736 | tf_op jit(solution)/shard_map/ppermute | solution.py:232
  96.2 0.0 copy-done
  96.2 5.2 %backward.1 = (bf16[128,1024]{1,0:T(8,128)(2,1)}, bf16[128,1024]{1,0:T(8,128)(2,1)}, bf16[128,1024]{1,0:T(8,128)(2,1)}, bf16[128,1024]{1,0:T(8,128)(2,1)}, bf16[...) custom-call(s32[1,4]{1,0:T(1,128)S(1)} %copy-done.2, ...), custom_call_target="tpu_custom_call" | custom-call | flops 1800000000 | bytes 9000000 | tf_op jit(solution)/shard_map/backward/pallas_call | solution.py:236
  101.4 0.0 collective-permute-done.1.source
  101.5 1.6 %finish.1 = (f32[1024,1024]{1,0:T(8,128)}, f32[2,1,512]{2,1,0:T(1,128)}) custom-call(bf16[4,1024,128]{2,1,0:T(8,128)(2,1)S(1)} %collective-permute-done.1.source, bf16[1024,1024]{1,0:T(8,128)(2,1)S(1)} %copy-done, f32[1,1024]{1,0:T(1,128)S(1)} %bitcast.7, f32[1024,1024]{1,0:T(8,128)} %get-tuple-element.29.weight_in, ...), custom_call_target="tpu_custom_call", output_to_operand_aliasing={{0}: (3, {}), {1}: (4, {})} | custom-call | flops 1500000 | bytes 4000000 | tf_op jit(solution)/shard_map/finish/pallas_call | solution.py:249
  (5 shorter events, 0.0 us)
Async XLA Ops:
  0.6 3.0 %copy-start.3 = (bf16[128,1024]{1,0:T(8,128)(2,1)S(1)}, bf16[128,1024]{1,0:T(8,128)(2,1)}, u32[]{:S(2)}) copy-start(bf16[128,1024]{1,0:T(8,128)(2,1)} %param.11) | copy-start | bytes 786436
  0.6 3.0 %copy-start.4 = (bf16[128,1024]{1,0:T(8,128)(2,1)S(1)}, bf16[128,1024]{1,0:T(8,128)(2,1)}, u32[]{:S(2)}) copy-start(bf16[128,1024]{1,0:T(8,128)(2,1)} %param.15) | copy-start | bytes 786436
  0.7 14.5 %copy-start.2 = (s32[1,4]{1,0:T(1,128)S(1)}, s32[1,4]{1,0:T(1,128)}, u32[]{:S(2)}) copy-start(s32[1,4]{1,0:T(1,128)} %lengths.3) | copy-start | bytes 52
  0.7 14.5 %copy-start.1 = (f32[1024]{0:T(1024)S(1)}, f32[1024]{0:T(1024)}, u32[]{:S(2)}) copy-start(f32[1024]{0:T(1024)} %param.13) | copy-start | bytes 12292
  3.7 11.4 %collective-permute-start = (bf16[640,1024]{1,0:T(8,128)(2,1)S(1)}, bf16[640,1024]{1,0:T(8,128)(2,1)S(1)}, u32[]{:S(2)}, u32[]{:S(2)}) collective-permute-start(bf16[640,1024]{1,0:T(8,128)(2,1)S(1)} %constant_dynamic-update-slice_fusion.own), channel_id=1, source_target_pairs={{0,1},{1,0},{2,3},{3,2},{4,5},{5,4},{6,7},{7,6},{8,9},{9,8},{10,11... | collective-permute-start | bytes 3932168 | tf_op jit(solution)/shard_map/ppermute | solution.py:194
  75.4 20.8 %copy-start = (bf16[1024,1024]{1,0:T(8,128)(2,1)S(1)}, bf16[1024,1024]{1,0:T(8,128)(2,1)}, u32[]{:S(2)}) copy-start(bf16[1024,1024]{1,0:T(8,128)(2,1)} %weight.3) | copy-start | bytes 6291460
  88.9 12.5 %collective-permute-start.1 = (bf16[4,1024,128]{2,1,0:T(8,128)(2,1)S(1)}, bf16[4,1024,128]{2,1,0:T(8,128)(2,1)S(1)}, u32[]{:S(2)}, u32[]{:S(2)}) collective-permute-start(bf16[4,1024,128]{2,1,0:T(8,128)(2,1)S(1)} %all_to_all.23.mine), channel_id=1, source_target_pairs={{0,1},{1,0},{2,3},{3,2},{4,5},{5,4},{6,7},{7,6},{8,9},{9,8},{10,11... | collective-permute-start | bytes 3145736 | tf_op jit(solution)/shard_map/ppermute | solution.py:232

commit v5 on v4

--- a/solution.py
+++ b/solution.py
@@ -12,7 +12,7 @@
 WIDTH = 1024
 ROWS = 128
 GROUP = 256
-PLANE = ("z", "y")
+PLANE = ("y", "z")
 CHIPS = ("z", "y", "x")
 DEVICES = ("z", "y", "x", "c")
 F32 = jnp.float32

time: 103 us -> 104 us (level)
  blocking collectives: 71.3 us -> 72.4 us
where the time goes in v5:
time: 104 us
  blocking collectives  72.4 us (70%)
  starting transfers between devices  15.4 us (15%)
  Pallas kernels  9.18 us (9%)
  local copies, waits for them, and re-layouts  3.16 us (3%)
  waiting for transfers between devices  2.64 us (3%)
    all_to_all x1, blocking collectives, per_device(): pieces = lax.all_to_all(block.reshape(64, 16, 128), PLANE, 0, 0, tiled=True)  24 us
    all_to_all x1, blocking collectives, per_device(): pieces = lax.all_to_all(part, 'x', 0, 0, tiled=True)  17.3 us
    all_to_all x1, blocking collectives, per_device(): block = lax.all_to_all(total, PLANE, 0, 0, tiled=True).reshape(1, 1024, 128)  17.3 us
    all_to_all x1, blocking collectives, per_device(): lax.all_to_all(jnp.broadcast_to(block, (4, 1024, 128)), 'x', 0, 0, tiled=...  13.9 us
    ppermute x1, starting transfers between devices, per_device(): other = lax.ppermute(own, 'c', swap)  8.79 us
    ppermute x1, starting transfers between devices, per_device(): theirs = lax.ppermute(mine, 'c', swap)  6.61 us
    pallas_call x1, Pallas kernels, per_device(): pl.pallas_call(backward_kernel, out_shape=[shape((ROWS, WIDTH), BF16)] *...  5.23 us
    unnamed x14, local copies, waits for them, and re-layouts  3 us
  transfers between devices with their start and end apart: 2, of which 1 were waited for; matrix products, arithmetic and copies ran while one was open for 0% of the time, Pallas kernels for 5%

profile of v5, /device:TPU:1, one launch (start us, length us, event | category | flops | bytes accessed | tf_op | source)
XLA Modules:
  0.0 103.6 jit_solution(2525146451529344127)
XLA Ops:
  0.6 0.0 copy-start.3
  0.6 0.0 copy-start.4
  0.7 0.0 copy-start.2
  0.7 0.0 copy-start.1
  0.7 1.0 constant_dynamic-update-slice_fusion.4
  1.7 1.0 constant_dynamic-update-slice_fusion.3
  2.7 1.0 constant_dynamic-update-slice_fusion.2
  3.6 0.0 copy-done.3
  3.7 8.8 %collective-permute-start = (bf16[640,1024]{1,0:T(8,128)(2,1)S(1)}, bf16[640,1024]{1,0:T(8,128)(2,1)S(1)}, u32[]{:S(2)}, u32[]{:S(2)}) collective-permute-start(bf16[640,1024]{1,0:T(8,128)(2,1)S(1)} %constant_dynamic-update-slice_fusion.own), channel_id=1, source_target_pairs={{0,1},{1,0},{2,3},{3,2},{4,5},{5,4},{6,7},{7,6},{8,9},{9,8},{10,11... | collective-permute-start | bytes 3932168 | tf_op jit(solution)/shard_map/ppermute | solution.py:194
  12.5 2.6 %collective-permute-done.other = bf16[640,1024]{1,0:T(8,128)(2,1)S(1)} collective-permute-done((bf16[640,1024]{1,0:T(8,128)(2,1)S(1)}, bf16[640,1024]{1,0:T(8,128)(2,1)S(1)}, u32[]{:S(2)}, u32[]{:S(2)}) %collective-permute-start) | collective-permute-done | bytes 1310752 | tf_op jit(solution)/shard_map/ppermute | solution.py:194
  15.2 0.0 copy-done.1
  15.2 2.1 %forward.1 = (bf16[4,1024,128]{2,1,0:T(8,128)(2,1)S(1)}, f32[256,1024]{1,0:T(8,128)S(1)}, f32[256,1]{1,0:T(8,128)S(1)}, bf16[128,1024]{1,0:T(8,128)(2,1)S(1)}) custom-call(s32[1,4]{1,0:T(1,128)S(1)} %copy-done.2, bf16[640,1024]{1,0:T(8,128)(2,1)S(1)} %constant_dynamic-update-slice_fusion.own, bf16[640,1024]{1,0:T(8,128)(2,1)S(1)} %collective-permute-done.other, ...), custom_call_target="tpu_custom_call" | custom-call | flops 540000000 | bytes 6000000 | tf_op jit(solution)/shard_map/forward/pallas_call | solution.py:195
  17.3 17.3 %all_to_all.20.pieces = bf16[4,1024,128]{2,1,0:T(8,128)(2,1)S(1)} all-to-all(bf16[4,1024,128]{2,1,0:T(8,128)(2,1)S(1)} %get-tuple-element.23), channel_id=1, replica_groups=mesh['z'=8,'y'=8,'x'=4,'c'=2] {'x'}, dimensions={0} | all-to-all | bytes 2097152 | tf_op jit(solution)/shard_map/all_to_all | solution.py:211
  34.6 0.1 chip_sum.1
  34.7 24.0 %all_to_all.21.pieces = bf16[64,16,128]{2,1,0:T(8,128)(2,1)S(1)} all-to-all(bf16[64,16,128]{2,1,0:T(8,128)(2,1)S(1)} %bitcast.4), channel_id=1, replica_groups=mesh['z'=8,'y'=8,'x'=4,'c'=2] {'y','z'}, dimensions={0} | all-to-all | bytes 524288 | tf_op jit(solution)/shard_map/all_to_all | solution.py:221
  58.7 0.1 plane_sum.1
  58.8 17.3 %all_to_all.22 = bf16[64,16,128]{2,1,0:T(8,128)(2,1)S(1)} all-to-all(bf16[64,16,128]{2,1,0:T(8,128)(2,1)S(1)} %plane_sum.1), channel_id=1, replica_groups=mesh['z'=8,'y'=8,'x'=4,'c'=2] {'y','z'}, dimensions={0} | all-to-all | bytes 524288 | tf_op jit(solution)/shard_map/all_to_all | solution.py:230
  76.0 0.1 broadcast_in_dim.8
  76.2 0.0 copy-start
  76.2 13.9 %all_to_all.23.mine = bf16[4,1024,128]{2,1,0:T(8,128)(2,1)S(1)} all-to-all(bf16[4,1024,128]{2,1,0:T(8,128)(2,1)S(1)} %broadcast_in_dim.8), channel_id=1, replica_groups=mesh['z'=8,'y'=8,'x'=4,'c'=2] {'x'}, dimensions={0} | all-to-all | bytes 2097152 | tf_op jit(solution)/shard_map/all_to_all | solution.py:231
  90.1 6.6 %collective-permute-start.1 = (bf16[4,1024,128]{2,1,0:T(8,128)(2,1)S(1)}, bf16[4,1024,128]{2,1,0:T(8,128)(2,1)S(1)}, u32[]{:S(2)}, u32[]{:S(2)}) collective-permute-start(bf16[4,1024,128]{2,1,0:T(8,128)(2,1)S(1)} %all_to_all.23.mine), channel_id=1, source_target_pairs={{0,1},{1,0},{2,3},{3,2},{4,5},{5,4},{6,7},{7,6},{8,9},{9,8},{10,11... | collective-permute-start | bytes 3145736 | tf_op jit(solution)/shard_map/ppermute | solution.py:232
  96.7 5.2 %backward.1 = (bf16[128,1024]{1,0:T(8,128)(2,1)}, bf16[128,1024]{1,0:T(8,128)(2,1)}, bf16[128,1024]{1,0:T(8,128)(2,1)}, bf16[128,1024]{1,0:T(8,128)(2,1)}, bf16[...) custom-call(s32[1,4]{1,0:T(1,128)S(1)} %copy-done.2, ...), custom_call_target="tpu_custom_call" | custom-call | flops 1800000000 | bytes 9000000 | tf_op jit(solution)/shard_map/backward/pallas_call | solution.py:236
  101.9 0.0 collective-permute-done.1.source
  102.0 1.6 %finish.1 = (f32[1024,1024]{1,0:T(8,128)}, f32[2,1,512]{2,1,0:T(1,128)}) custom-call(bf16[4,1024,128]{2,1,0:T(8,128)(2,1)S(1)} %collective-permute-done.1.source, bf16[1024,1024]{1,0:T(8,128)(2,1)S(1)} %copy-done, f32[1,1024]{1,0:T(1,128)S(1)} %bitcast.7, f32[1024,1024]{1,0:T(8,128)} %get-tuple-element.29.weight_in, ...), custom_call_target="tpu_custom_call", output_to_operand_aliasing={{0}: (3, {}), {1}: (4, {})} | custom-call | flops 1500000 | bytes 4000000 | tf_op jit(solution)/shard_map/finish/pallas_call | solution.py:249
  (5 shorter events, 0.0 us)
Async XLA Ops:
  0.6 3.0 %copy-start.3 = (bf16[128,1024]{1,0:T(8,128)(2,1)S(1)}, bf16[128,1024]{1,0:T(8,128)(2,1)}, u32[]{:S(2)}) copy-start(bf16[128,1024]{1,0:T(8,128)(2,1)} %param.11) | copy-start | bytes 786436
  0.6 3.0 %copy-start.4 = (bf16[128,1024]{1,0:T(8,128)(2,1)S(1)}, bf16[128,1024]{1,0:T(8,128)(2,1)}, u32[]{:S(2)}) copy-start(bf16[128,1024]{1,0:T(8,128)(2,1)} %param.15) | copy-start | bytes 786436
  0.7 14.5 %copy-start.2 = (s32[1,4]{1,0:T(1,128)S(1)}, s32[1,4]{1,0:T(1,128)}, u32[]{:S(2)}) copy-start(s32[1,4]{1,0:T(1,128)} %lengths.3) | copy-start | bytes 52
  0.7 14.5 %copy-start.1 = (f32[1024]{0:T(1024)S(1)}, f32[1024]{0:T(1024)}, u32[]{:S(2)}) copy-start(f32[1024]{0:T(1024)} %param.13) | copy-start | bytes 12292
  3.7 11.4 %collective-permute-start = (bf16[640,1024]{1,0:T(8,128)(2,1)S(1)}, bf16[640,1024]{1,0:T(8,128)(2,1)S(1)}, u32[]{:S(2)}, u32[]{:S(2)}) collective-permute-start(bf16[640,1024]{1,0:T(8,128)(2,1)S(1)} %constant_dynamic-update-slice_fusion.own), channel_id=1, source_target_pairs={{0,1},{1,0},{2,3},{3,2},{4,5},{5,4},{6,7},{7,6},{8,9},{9,8},{10,11... | collective-permute-start | bytes 3932168 | tf_op jit(solution)/shard_map/ppermute | solution.py:194
  76.2 20.5 %copy-start = (bf16[1024,1024]{1,0:T(8,128)(2,1)S(1)}, bf16[1024,1024]{1,0:T(8,128)(2,1)}, u32[]{:S(2)}) copy-start(bf16[1024,1024]{1,0:T(8,128)(2,1)} %weight.3) | copy-start | bytes 6291460
  90.1 11.9 %collective-permute-start.1 = (bf16[4,1024,128]{2,1,0:T(8,128)(2,1)S(1)}, bf16[4,1024,128]{2,1,0:T(8,128)(2,1)S(1)}, u32[]{:S(2)}, u32[]{:S(2)}) collective-permute-start(bf16[4,1024,128]{2,1,0:T(8,128)(2,1)S(1)} %all_to_all.23.mine), channel_id=1, source_target_pairs={{0,1},{1,0},{2,3},{3,2},{4,5},{5,4},{6,7},{7,6},{8,9},{9,8},{10,11... | collective-permute-start | bytes 3145736 | tf_op jit(solution)/shard_map/ppermute | solution.py:232
